TPU v7x, 512 devices: a whole 4x8x8 slice. The times are simulated.
512 devices in a mesh: lon: 64 (over y, z_hi, core), lat: 8 (over x, z_lo).
Axes of the slice: x: 4, y: 8, z: 8 (z_hi: 4, z_lo: 2; z = z_hi * 2 + z_lo), core: 2. Of those that a mesh axis runs over, the one named last changes fastest.
Arguments:
- field: bfloat16 [96, 128, 8192], P(None, 'lat', 'lon'), may hold values from -6 to 6
- land_mask: int32 [128, 8192], P('lat', 'lon'), may hold values from 0 to 1, as said below
- depth_kernel: float32 [2, 96, 7, 7], replicated, may hold values from -0.875 to 0.875
- depth_bias: float32 [2, 96], replicated, may hold values from -3 to 3
- norm_gain: float32 [2, 96], replicated, may hold values from 0.1 to 1.9
- norm_bias: float32 [2, 96], replicated, may hold values from -3 to 3
- w_expand: bfloat16 [2, 384, 96], replicated, may hold values from -0.625 to 0.625
- b_expand: float32 [2, 384], replicated, may hold values from -3 to 3
- w_reduce: bfloat16 [2, 96, 384], replicated, may hold values from -0.3125 to 0.3125
- b_reduce: float32 [2, 96], replicated, may hold values from -3 to 3
Outputs:
- output_field: bfloat16 [96, 128, 8192], P(None, 'lat', 'lon')
Inputs may be any that keep to these rules, and one draw needn't show every extreme that they name: `land_mask`: land and ocean come in regions; some aligned blocks of 8 rows and 128 columns are all land.
All inputs are finite; a program needn't handle non-finite values.
Results may differ from a plain program's by a relative error of at most 0.0058.
Values may be sent and summed in bfloat16 or wider, within the bound.
A program may use at most 64 MiB of HBM per device.

v0:
```python
import jax
import jax.numpy as jnp
from jax import lax
from jax.sharding import PartitionSpec as P

LAYERS = 2


def extended_2(value, sides, width, wrap):
    for axis, dim in sides:
        count, length = (lax.axis_size(axis), value.shape[dim])
        up = [(i, (i + 1) % count) for i in range(count if wrap else count - 1)]
        down = [(j, i) for i, j in up]
        last = lax.slice_in_dim(value, length - width, length, axis=dim)
        leading = lax.slice_in_dim(value, 0, width, axis=dim)
        before = lax.ppermute(last, axis, up)
        after = lax.ppermute(leading, axis, down)
        value = jnp.concatenate([before, value, after], axis=dim)
    return value


def depthwise(band_rows, kernel, conv_bias):
    band_rows = band_rows.astype(jnp.float32)
    height = band_rows.shape[1] - 6
    width = band_rows.shape[2] - 6
    summed = jnp.zeros((band_rows.shape[0], height, width), jnp.float32) + conv_bias[:, None, None]
    for shift_row in range(7):
        for shift_col in range(7):
            summed = (
                summed
                + kernel[:, shift_row, shift_col, None, None]
                * band_rows[:, shift_row : shift_row + height, shift_col : shift_col + width]
            )
    return summed


def finish(
    mixed_cells,
    old_values,
    ocean_flags,
    norm_gain,
    norm_bias,
    w_expand,
    b_expand,
    w_reduce,
    b_reduce,
):
    channels, height, width = mixed_cells.shape
    flat_cells = mixed_cells.reshape(channels, height * width)
    average = jnp.mean(flat_cells, axis=0)
    centered = flat_cells - average
    variance = jnp.mean(centered * centered, axis=0)
    normed = (
        centered / jnp.sqrt(variance + 1e-06) * norm_gain[:, None] + norm_bias[:, None]
    ).astype(jnp.bfloat16)
    hidden = jnp.dot(w_expand, normed, preferred_element_type=jnp.float32) + b_expand[:, None]
    hidden = jax.nn.gelu(hidden, approximate=False).astype(jnp.bfloat16)
    update = jnp.dot(w_reduce, hidden, preferred_element_type=jnp.float32) + b_reduce[:, None]
    flags = ocean_flags.reshape(height * width).astype(jnp.float32)
    result_band = flags[None, :] * (
        old_values.reshape(channels, height * width).astype(jnp.float32) + update
    )
    return result_band.astype(jnp.bfloat16).reshape(channels, height, width)


def convnext_layer(
    values,
    land_mask,
    kernel,
    conv_bias,
    norm_gain,
    norm_bias,
    w_expand,
    b_expand,
    w_reduce,
    b_reduce,
):
    own_strip = values[:, -3:, :][:, ::-1, ::-1]
    tiles = lax.axis_size("lon")
    pieces = own_strip.reshape(tiles, own_strip.size // tiles)
    spread = lax.all_to_all(pieces, "lon", split_axis=0, concat_axis=0, tiled=True)
    spread = spread[::-1]
    collected = lax.all_to_all(spread, "lon", split_axis=0, concat_axis=0, tiled=True)
    fold_rows = collected.reshape(own_strip.shape)
    extended = extended_2(values, (("lat", 1),), 3, False)
    at_top = lax.axis_index("lat") == lax.axis_size("lat") - 1
    upper_rows = jnp.where(at_top, fold_rows, extended[:, -3:, :])
    extended = jnp.concatenate([extended[:, :-3, :], upper_rows], axis=1)
    extended = extended_2(extended, (("lon", 2),), 3, True)
    mixed_all = depthwise(extended, kernel, conv_bias)

    def band_step(band, result):
        start = band * 8
        mixed_cells = lax.dynamic_slice_in_dim(mixed_all, start, 8, 1)
        old_values = lax.dynamic_slice_in_dim(values, start, 8, 1)
        ocean_flags = lax.dynamic_slice_in_dim(land_mask, start, 8, 0)
        result_band = finish(
            mixed_cells,
            old_values,
            ocean_flags,
            norm_gain,
            norm_bias,
            w_expand,
            b_expand,
            w_reduce,
            b_reduce,
        )
        return lax.dynamic_update_slice_in_dim(result, result_band, start, 1)

    blank = jnp.zeros(values.shape, jnp.bfloat16)
    return lax.fori_loop(0, values.shape[1] // 8, band_step, blank)


def per_device(
    field,
    land_mask,
    depth_kernel,
    depth_bias,
    norm_gain,
    norm_bias,
    w_expand,
    b_expand,
    w_reduce,
    b_reduce,
):
    values = field
    for layer_index in range(LAYERS):
        values = convnext_layer(
            values,
            land_mask,
            depth_kernel[layer_index],
            depth_bias[layer_index],
            norm_gain[layer_index],
            norm_bias[layer_index],
            w_expand[layer_index],
            b_expand[layer_index],
            w_reduce[layer_index],
            b_reduce[layer_index],
        )
    return values


def solution(mesh):
    placed = (P(None, "lat", "lon"), P("lat", "lon"), P(), P(), P(), P(), P(), P(), P(), P())
    return jax.shard_map(
        per_device, mesh=mesh, in_specs=placed, out_specs=P(None, "lat", "lon"), check_vma=False
    )
```

profile of v0, /device:TPU:6, one launch (start us, length us, event | category | flops | bytes accessed | tf_op | source)
XLA Modules:
  0.0 161.6 jit_solution(8692409053611672619)
XLA Ops:
  0.0 1.7 %copy.36 = bf16[96,16,128]{0,1,2:T(8,128)(2,1)S(1)} copy(bf16[96,16,128]{2,1,0:T(8,128)(2,1)} %param.14) | data formatting | bytes 786432 | tf_op args[0]
  1.8 4.3 %collective-permute-start = (bf16[96,3,128]{0,1,2:T(4,128)(2,1)S(1)}, bf16[96,3,128]{0,1,2:T(4,128)(2,1)S(1)}, u32[]{:S(2)}, u32[]{:S(2)}) collective-permute-start(bf16[96,3,128]{0,1,2:T(4,128)(2,1)S(1)} %slice.883), channel_id=1, source_target_pairs={{0,1},{1,2},{2,3},{3,4},{4,5},{5,6},{6,7},{8,9},{9,10},{10,11},{11... | collective-permute-start | bytes 221192 | tf_op jit(solution)/shard_map/ppermute | solution.py:16
  7.2 1.0 reduce.16
  8.2 0.8 reshape.170
  9.0 15.7 %all-to-all-start = ((bf16[64,2,288]{2,1,0:T(2,128)(2,1)}), bf16[64,2,288]{2,1,0:T(2,128)(2,1)S(1)}, u32[]{:S(2)}, u32[]{:S(2)}) async-start(bf16[64,2,288]{2,1,0:T(2,128)(2,1)} %reshape.170), calls=%async_computation | async-start | bytes 196608 | tf_op jit(solution)/shard_map/all_to_all | solution.py:81
  24.7 3.4 %collective-permute-start.1 = (bf16[96,3,128]{2,1,0:T(4,128)(2,1)S(1)}, bf16[96,3,128]{2,1,0:T(4,128)(2,1)S(1)}, u32[]{:S(2)}, u32[]{:S(2)}) collective-permute-start(bf16[96,3,128]{2,1,0:T(4,128)(2,1)S(1)} %slice.666), channel_id=1, source_target_pairs={{1,0},{2,1},{3,2},{4,3},{5,4},{6,5},{7,6},{9,8},{10,9},{11,10},{12... | collective-permute-start | bytes 221192 | tf_op jit(solution)/shard_map/ppermute | solution.py:17
  28.4 9.2 %all-to-all-done = bf16[64,2,288]{2,1,0:T(2,128)(2,1)S(1)} async-done(((bf16[64,2,288]{2,1,0:T(2,128)(2,1)}), bf16[64,2,288]{2,1,0:T(2,128)(2,1)S(1)}, u32[]{:S(2)}, u32[]{:S(2)}) %all-to-all-start) | async-done | bytes 73760 | tf_op jit(solution)/shard_map/all_to_all | solution.py:81
  38.5 0.8 reshape.172
  39.3 4.6 %all-to-all-start.1 = ((bf16[64,2,288]{2,1,0:T(2,128)(2,1)}), bf16[64,2,288]{2,1,0:T(2,128)(2,1)S(1)}, u32[]{:S(2)}, u32[]{:S(2)}) async-start(bf16[64,2,288]{2,1,0:T(2,128)(2,1)} %reshape.172), calls=%async_computation.1 | async-start | bytes 196608 | tf_op jit(solution)/shard_map/all_to_all | solution.py:83
  44.0 12.9 %all-to-all-done.1 = bf16[64,2,288]{2,1,0:T(2,128)(2,1)S(1)} async-done(((bf16[64,2,288]{2,1,0:T(2,128)(2,1)}), bf16[64,2,288]{2,1,0:T(2,128)(2,1)S(1)}, u32[]{:S(2)}, u32[]{:S(2)}) %all-to-all-start.1) | async-done | bytes 73760 | tf_op jit(solution)/shard_map/all_to_all | solution.py:83
  58.0 2.0 %collective-permute-start.2 = (bf16[96,22,3]{0,1,2:T(8,128)(2,1)S(1)}, bf16[96,22,3]{0,1,2:T(8,128)(2,1)S(1)}, u32[]{:S(2)}, u32[]{:S(2)}) collective-permute-start(bf16[96,22,3]{0,1,2:T(8,128)(2,1)S(1)} %get-tuple-element.473), channel_id=1, source_target_pairs={{0,8},{8,16},{16,24},{24,32},{32,40},{40,48},{48,56},{56,64},{64,7... | collective-permute-start | bytes 38024 | tf_op jit(solution)/shard_map/ppermute | solution.py:16
  60.0 7.9 %collective-permute-start.3 = (bf16[96,22,3]{0,1,2:T(8,128)(2,1)S(1)}, bf16[96,22,3]{0,1,2:T(8,128)(2,1)S(1)}, u32[]{:S(2)}, u32[]{:S(2)}) collective-permute-start(bf16[96,22,3]{0,1,2:T(8,128)(2,1)S(1)} %get-tuple-element.474), channel_id=1, source_target_pairs={{8,0},{16,8},{24,16},{32,24},{40,32},{48,40},{56,48},{64,56},{72,6... | collective-permute-start | bytes 38024 | tf_op jit(solution)/shard_map/ppermute | solution.py:17
  68.1 1.1 collective-permute-done.3
  69.6 7.8 %fusion.251 = f32[96,16,128]{0,1,2:T(8,128)S(1)} fusion(f32[96,22,134]{0,1,2:T(8,128)S(1)} %maximum_convert_fusion, f32[96]{0:T(128)S(1)} %get-tuple-element.531, f32[96]{0:T(128)S(1)} %get-tuple-element.532, f32[96]{0:T(128)S(1)} %get-tuple-element.533, f32[96]{0:T(128)S(1)} %get-tuple-element.534, f32[96]{0:T(128)S(1)} %get-tuple-element.535, ...), kind=kLoop, calls=%fused_computation.317 | loop fusion | flops 19267584 | bytes 39340800 | tf_op jit(solution)/shard_map/add | solution.py:30
  78.1 9.0 %while.26 = (s32[]{:T(128)}, bf16[96,16,128]{2,1,0:T(8,128)(2,1)S(1)}, s32[16,128]{1,0:T(8,128)S(1)}, bf16[96,16,128]{2,1,0:T(8,128)(2,1)S(1)}, f32[96,16,128]{2...) while((s32[]{:T(128)}, ...), condition=%wide.region_3.4_spmd, body=%wide.region_0.3_spmd.sunk | while | flops 178325504 | bytes 3745623 | solution.py:111
  78.5 4.1 %fusion.329 = bf16[12,8,8,128]{3,1,2,0:T(8,128)(2,1)S(1)} fusion(bf16[96,384]{1,0:T(8,128)(2,1)S(1)} %get-tuple-element.784, bf16[384,96]{1,0:T(8,128)(2,1)S(1)} %get-tuple-element.782, f32[384]{0:T(512)S(1)} %reduce.22, f32[12,8,8,128]{3,2,1,0:T(8,128)S(1)} %bitcast.552, f32[12,8,8,128]{3,2,1,0:T(8,128)S(1)} %bitcast.548, f32[96]{0:T(128)S(1)} %bitcast.564, ...), kind=kOutput, calls=%fused_computation.30.clone.1 | convolution fusion | flops 177831936 | bytes 1145472 | tf_op jit(solution)/shard_map/while/body/eval_jaxpr/dot_general | solution.py:58
  83.0 4.1 %fusion.329 = bf16[12,8,8,128]{3,1,2,0:T(8,128)(2,1)S(1)} fusion(bf16[96,384]{1,0:T(8,128)(2,1)S(1)} %get-tuple-element.784, bf16[384,96]{1,0:T(8,128)(2,1)S(1)} %get-tuple-element.782, f32[384]{0:T(512)S(1)} %reduce.22, f32[12,8,8,128]{3,2,1,0:T(8,128)S(1)} %bitcast.552, f32[12,8,8,128]{3,2,1,0:T(8,128)S(1)} %bitcast.548, f32[96]{0:T(128)S(1)} %bitcast.564, ...), kind=kOutput, calls=%fused_computation.30.clone.1 | convolution fusion | flops 177831936 | bytes 1145472 | tf_op jit(solution)/shard_map/while/body/eval_jaxpr/dot_general | solution.py:58
  88.4 1.1 reduce.18
  89.4 0.8 reshape.174
  90.2 8.2 %all-to-all-start.2 = ((bf16[64,2,288]{2,1,0:T(2,128)(2,1)}), bf16[64,2,288]{2,1,0:T(2,128)(2,1)S(1)}, u32[]{:S(2)}, u32[]{:S(2)}) async-start(bf16[64,2,288]{2,1,0:T(2,128)(2,1)} %reshape.174), calls=%async_computation.2 | async-start | bytes 196608 | tf_op jit(solution)/shard_map/all_to_all | solution.py:81
  98.5 3.4 %collective-permute-start.5 = (bf16[96,3,128]{2,1,0:T(4,128)(2,1)S(1)}, bf16[96,3,128]{2,1,0:T(4,128)(2,1)S(1)}, u32[]{:S(2)}, u32[]{:S(2)}) collective-permute-start(bf16[96,3,128]{2,1,0:T(4,128)(2,1)S(1)} %slice.776), channel_id=1, source_target_pairs={{1,0},{2,1},{3,2},{4,3},{5,4},{6,5},{7,6},{9,8},{10,9},{11,10},{12... | collective-permute-start | bytes 221192 | tf_op jit(solution)/shard_map/ppermute | solution.py:17
  101.9 9.5 %all-to-all-done.2 = bf16[64,2,288]{2,1,0:T(2,128)(2,1)S(1)} async-done(((bf16[64,2,288]{2,1,0:T(2,128)(2,1)}), bf16[64,2,288]{2,1,0:T(2,128)(2,1)S(1)}, u32[]{:S(2)}, u32[]{:S(2)}) %all-to-all-start.2) | async-done | bytes 73760 | tf_op jit(solution)/shard_map/all_to_all | solution.py:81
  113.1 4.6 %all-to-all-start.3 = ((bf16[64,2,288]{2,1,0:T(2,128)(2,1)}), bf16[64,2,288]{2,1,0:T(2,128)(2,1)S(1)}, u32[]{:S(2)}, u32[]{:S(2)}) async-start(bf16[64,2,288]{2,1,0:T(2,128)(2,1)} %reshape.176), calls=%async_computation.3 | async-start | bytes 196608 | tf_op jit(solution)/shard_map/all_to_all | solution.py:83
  117.7 2.1 %collective-permute-start.4 = (bf16[96,3,128]{0,1,2:T(4,128)(2,1)S(1)}, bf16[96,3,128]{0,1,2:T(4,128)(2,1)S(1)}, u32[]{:S(2)}, u32[]{:S(2)}) collective-permute-start(bf16[96,3,128]{0,1,2:T(4,128)(2,1)S(1)} %slice.982), channel_id=1, source_target_pairs={{0,1},{1,2},{2,3},{3,4},{4,5},{5,6},{6,7},{8,9},{9,10},{10,11},{11... | collective-permute-start | bytes 221192 | tf_op jit(solution)/shard_map/ppermute | solution.py:16
  119.9 10.8 %all-to-all-done.3 = bf16[64,2,288]{2,1,0:T(2,128)(2,1)S(1)} async-done(((bf16[64,2,288]{2,1,0:T(2,128)(2,1)}), bf16[64,2,288]{2,1,0:T(2,128)(2,1)S(1)}, u32[]{:S(2)}, u32[]{:S(2)}) %all-to-all-start.3) | async-done | bytes 73760 | tf_op jit(solution)/shard_map/all_to_all | solution.py:83
  131.7 2.0 %collective-permute-start.6 = (bf16[96,22,3]{0,1,2:T(8,128)(2,1)S(1)}, bf16[96,22,3]{0,1,2:T(8,128)(2,1)S(1)}, u32[]{:S(2)}, u32[]{:S(2)}) collective-permute-start(bf16[96,22,3]{0,1,2:T(8,128)(2,1)S(1)} %get-tuple-element.471), channel_id=1, source_target_pairs={{0,8},{8,16},{16,24},{24,32},{32,40},{40,48},{48,56},{56,64},{64,7... | collective-permute-start | bytes 38024 | tf_op jit(solution)/shard_map/ppermute | solution.py:16
  133.8 7.8 %collective-permute-start.7 = (bf16[96,22,3]{0,1,2:T(8,128)(2,1)S(1)}, bf16[96,22,3]{0,1,2:T(8,128)(2,1)S(1)}, u32[]{:S(2)}, u32[]{:S(2)}) collective-permute-start(bf16[96,22,3]{0,1,2:T(8,128)(2,1)S(1)} %get-tuple-element.472), channel_id=1, source_target_pairs={{8,0},{16,8},{24,16},{32,24},{40,32},{48,40},{56,48},{64,56},{72,6... | collective-permute-start | bytes 38024 | tf_op jit(solution)/shard_map/ppermute | solution.py:17
  141.7 1.3 collective-permute-done.7
  143.4 7.8 %fusion.202 = f32[96,16,128]{0,1,2:T(8,128)S(1)} fusion(f32[96,22,134]{0,1,2:T(8,128)S(1)} %maximum_convert_fusion.1, f32[96]{0:T(128)S(1)} %get-tuple-element.482, f32[96]{0:T(128)S(1)} %get-tuple-element.483, f32[96]{0:T(128)S(1)} %get-tuple-element.484, f32[96]{0:T(128)S(1)} %get-tuple-element.485, f32[96]{0:T(128)S(1)} %get-tuple-element.486, ...), kind=kLoop, calls=%fused_computation.219 | loop fusion | flops 19267584 | bytes 39340800 | tf_op jit(solution)/shard_map/add | solution.py:30
  151.9 9.0 %while.27 = (s32[]{:T(128)}, bf16[96,16,128]{2,1,0:T(8,128)(2,1)S(1)}, s32[16,128]{1,0:T(8,128)S(1)}, bf16[96,16,128]{2,1,0:T(8,128)(2,1)S(1)}, f32[96,16,128]{2...) while((s32[]{:T(128)}, ...), condition=%wide.region_7.8_spmd, body=%wide.region_4.7_spmd.sunk | while | flops 178325504 | bytes 3745623 | solution.py:111
  152.2 4.1 %fusion.335 = bf16[12,8,8,128]{3,1,2,0:T(8,128)(2,1)S(1)} fusion(bf16[96,384]{1,0:T(8,128)(2,1)S(1)} %get-tuple-element.832, bf16[384,96]{1,0:T(8,128)(2,1)S(1)} %get-tuple-element.830, f32[384]{0:T(512)S(1)} %reduce.23, f32[12,8,8,128]{3,2,1,0:T(8,128)S(1)} %bitcast.553, f32[12,8,8,128]{3,2,1,0:T(8,128)S(1)} %bitcast.549, f32[96]{0:T(128)S(1)} %bitcast.562, ...), kind=kOutput, calls=%fused_computation.139.clone.1 | convolution fusion | flops 177831936 | bytes 1145472 | tf_op jit(solution)/shard_map/while/body/eval_jaxpr/dot_general | solution.py:58
  156.7 4.1 %fusion.335 = bf16[12,8,8,128]{3,1,2,0:T(8,128)(2,1)S(1)} fusion(bf16[96,384]{1,0:T(8,128)(2,1)S(1)} %get-tuple-element.832, bf16[384,96]{1,0:T(8,128)(2,1)S(1)} %get-tuple-element.830, f32[384]{0:T(512)S(1)} %reduce.23, f32[12,8,8,128]{3,2,1,0:T(8,128)S(1)} %bitcast.553, f32[12,8,8,128]{3,2,1,0:T(8,128)S(1)} %bitcast.549, f32[96]{0:T(128)S(1)} %bitcast.562, ...), kind=kOutput, calls=%fused_computation.139.clone.1 | convolution fusion | flops 177831936 | bytes 1145472 | tf_op jit(solution)/shard_map/while/body/eval_jaxpr/dot_general | solution.py:58
  (119 shorter events, 12.0 us)
Async XLA Ops:
  0.0 24.7 %copy-start = (bf16[96,16,128]{2,1,0:T(8,128)(2,1)S(1)}, bf16[96,16,128]{2,1,0:T(8,128)(2,1)}, u32[]{:S(2)}) copy-start(bf16[96,16,128]{2,1,0:T(8,128)(2,1)} %param.14) | copy-start | bytes 1179652
  0.0 28.1 %copy-start.5 = (f32[2,96,7,7]{1,0,3,2:T(2,128)S(1)}, f32[2,96,7,7]{1,0,3,2:T(2,128)}, u32[]{:S(2)}) copy-start(f32[2,96,7,7]{1,0,3,2:T(2,128)} %param.16) | copy-start | bytes 112900
  0.0 28.2 %copy-start.3 = (bf16[2,384,96]{1,2,0:T(8,128)(2,1)S(1)}, bf16[2,384,96]{1,2,0:T(8,128)(2,1)}, u32[]{:S(2)}) copy-start(bf16[2,384,96]{1,2,0:T(8,128)(2,1)} %param.20) | copy-start | bytes 442372
  0.0 28.3 %copy-start.4 = (bf16[2,96,384]{2,1,0:T(8,128)(2,1)S(1)}, bf16[2,96,384]{2,1,0:T(8,128)(2,1)}, u32[]{:S(2)}) copy-start(bf16[2,96,384]{2,1,0:T(8,128)(2,1)} %param.22) | copy-start | bytes 442372
  1.7 26.6 %copy-start.6 = (f32[2,384]{1,0:T(2,128)S(1)}, f32[2,384]{1,0:T(2,128)}, u32[]{:S(2)}) copy-start(f32[2,384]{1,0:T(2,128)} %param.21) | copy-start | bytes 9220
  1.7 26.6 %copy-start.9 = (f32[2,96]{1,0:T(2,128)S(1)}, f32[2,96]{1,0:T(2,128)}, u32[]{:S(2)}) copy-start(f32[2,96]{1,0:T(2,128)} %param.23) | copy-start | bytes 2308
  1.7 26.6 %copy-start.10 = (f32[2,96]{1,0:T(2,128)S(1)}, f32[2,96]{1,0:T(2,128)}, u32[]{:S(2)}) copy-start(f32[2,96]{1,0:T(2,128)} %param.19) | copy-start | bytes 2308
  1.8 56.1 %collective-permute-start = (bf16[96,3,128]{0,1,2:T(4,128)(2,1)S(1)}, bf16[96,3,128]{0,1,2:T(4,128)(2,1)S(1)}, u32[]{:S(2)}, u32[]{:S(2)}) collective-permute-start(bf16[96,3,128]{0,1,2:T(4,128)(2,1)S(1)} %slice.883), channel_id=1, source_target_pairs={{0,1},{1,2},{2,3},{3,4},{4,5},{5,6},{6,7},{8,9},{9,10},{10,11},{11... | collective-permute-start | bytes 221192 | tf_op jit(solution)/shard_map/ppermute | solution.py:16
  6.5 37.4 %copy-start.7 = (f32[2,96]{1,0:T(2,128)S(1)}, f32[2,96]{1,0:T(2,128)}, u32[]{:S(2)}) copy-start(f32[2,96]{1,0:T(2,128)} %param.17) | copy-start | bytes 2308
  9.0 28.6 %all-to-all-start = ((bf16[64,2,288]{2,1,0:T(2,128)(2,1)}), bf16[64,2,288]{2,1,0:T(2,128)(2,1)S(1)}, u32[]{:S(2)}, u32[]{:S(2)}) async-start(bf16[64,2,288]{2,1,0:T(2,128)(2,1)} %reshape.170), calls=%async_computation | async-start | bytes 196608 | tf_op jit(solution)/shard_map/all_to_all | solution.py:81
  24.7 33.0 %collective-permute-start.1 = (bf16[96,3,128]{2,1,0:T(4,128)(2,1)S(1)}, bf16[96,3,128]{2,1,0:T(4,128)(2,1)S(1)}, u32[]{:S(2)}, u32[]{:S(2)}) collective-permute-start(bf16[96,3,128]{2,1,0:T(4,128)(2,1)S(1)} %slice.666), channel_id=1, source_target_pairs={{1,0},{2,1},{3,2},{4,3},{5,4},{6,5},{7,6},{9,8},{10,9},{11,10},{12... | collective-permute-start | bytes 221192 | tf_op jit(solution)/shard_map/ppermute | solution.py:17
  28.4 39.6 %copy-start.8 = (f32[2,96]{1,0:T(2,128)S(1)}, f32[2,96]{1,0:T(2,128)}, u32[]{:S(2)}) copy-start(f32[2,96]{1,0:T(2,128)} %param.18) | copy-start | bytes 2308
  39.3 17.6 %all-to-all-start.1 = ((bf16[64,2,288]{2,1,0:T(2,128)(2,1)}), bf16[64,2,288]{2,1,0:T(2,128)(2,1)S(1)}, u32[]{:S(2)}, u32[]{:S(2)}) async-start(bf16[64,2,288]{2,1,0:T(2,128)(2,1)} %reshape.172), calls=%async_computation.1 | async-start | bytes 196608 | tf_op jit(solution)/shard_map/all_to_all | solution.py:83
  58.0 10.1 %collective-permute-start.2 = (bf16[96,22,3]{0,1,2:T(8,128)(2,1)S(1)}, bf16[96,22,3]{0,1,2:T(8,128)(2,1)S(1)}, u32[]{:S(2)}, u32[]{:S(2)}) collective-permute-start(bf16[96,22,3]{0,1,2:T(8,128)(2,1)S(1)} %get-tuple-element.473), channel_id=1, source_target_pairs={{0,8},{8,16},{16,24},{24,32},{32,40},{40,48},{48,56},{56,64},{64,7... | collective-permute-start | bytes 38024 | tf_op jit(solution)/shard_map/ppermute | solution.py:16
  60.0 9.2 %collective-permute-start.3 = (bf16[96,22,3]{0,1,2:T(8,128)(2,1)S(1)}, bf16[96,22,3]{0,1,2:T(8,128)(2,1)S(1)}, u32[]{:S(2)}, u32[]{:S(2)}) collective-permute-start(bf16[96,22,3]{0,1,2:T(8,128)(2,1)S(1)} %get-tuple-element.474), channel_id=1, source_target_pairs={{8,0},{16,8},{24,16},{32,24},{40,32},{48,40},{56,48},{64,56},{72,6... | collective-permute-start | bytes 38024 | tf_op jit(solution)/shard_map/ppermute | solution.py:17
  77.4 0.7 copy-start.2
  90.2 21.1 %all-to-all-start.2 = ((bf16[64,2,288]{2,1,0:T(2,128)(2,1)}), bf16[64,2,288]{2,1,0:T(2,128)(2,1)S(1)}, u32[]{:S(2)}, u32[]{:S(2)}) async-start(bf16[64,2,288]{2,1,0:T(2,128)(2,1)} %reshape.174), calls=%async_computation.2 | async-start | bytes 196608 | tf_op jit(solution)/shard_map/all_to_all | solution.py:81
  98.5 32.9 %collective-permute-start.5 = (bf16[96,3,128]{2,1,0:T(4,128)(2,1)S(1)}, bf16[96,3,128]{2,1,0:T(4,128)(2,1)S(1)}, u32[]{:S(2)}, u32[]{:S(2)}) collective-permute-start(bf16[96,3,128]{2,1,0:T(4,128)(2,1)S(1)} %slice.776), channel_id=1, source_target_pairs={{1,0},{2,1},{3,2},{4,3},{5,4},{6,5},{7,6},{9,8},{10,9},{11,10},{12... | collective-permute-start | bytes 221192 | tf_op jit(solution)/shard_map/ppermute | solution.py:17
  113.1 17.6 %all-to-all-start.3 = ((bf16[64,2,288]{2,1,0:T(2,128)(2,1)}), bf16[64,2,288]{2,1,0:T(2,128)(2,1)S(1)}, u32[]{:S(2)}, u32[]{:S(2)}) async-start(bf16[64,2,288]{2,1,0:T(2,128)(2,1)} %reshape.176), calls=%async_computation.3 | async-start | bytes 196608 | tf_op jit(solution)/shard_map/all_to_all | solution.py:83
  117.7 14.0 %collective-permute-start.4 = (bf16[96,3,128]{0,1,2:T(4,128)(2,1)S(1)}, bf16[96,3,128]{0,1,2:T(4,128)(2,1)S(1)}, u32[]{:S(2)}, u32[]{:S(2)}) collective-permute-start(bf16[96,3,128]{0,1,2:T(4,128)(2,1)S(1)} %slice.982), channel_id=1, source_target_pairs={{0,1},{1,2},{2,3},{3,4},{4,5},{5,6},{6,7},{8,9},{9,10},{10,11},{11... | collective-permute-start | bytes 221192 | tf_op jit(solution)/shard_map/ppermute | solution.py:16
  131.7 9.9 %collective-permute-start.6 = (bf16[96,22,3]{0,1,2:T(8,128)(2,1)S(1)}, bf16[96,22,3]{0,1,2:T(8,128)(2,1)S(1)}, u32[]{:S(2)}, u32[]{:S(2)}) collective-permute-start(bf16[96,22,3]{0,1,2:T(8,128)(2,1)S(1)} %get-tuple-element.471), channel_id=1, source_target_pairs={{0,8},{8,16},{16,24},{24,32},{32,40},{40,48},{48,56},{56,64},{64,7... | collective-permute-start | bytes 38024 | tf_op jit(solution)/shard_map/ppermute | solution.py:16
  133.8 9.2 %collective-permute-start.7 = (bf16[96,22,3]{0,1,2:T(8,128)(2,1)S(1)}, bf16[96,22,3]{0,1,2:T(8,128)(2,1)S(1)}, u32[]{:S(2)}, u32[]{:S(2)}) collective-permute-start(bf16[96,22,3]{0,1,2:T(8,128)(2,1)S(1)} %get-tuple-element.472), channel_id=1, source_target_pairs={{8,0},{16,8},{24,16},{32,24},{40,32},{48,40},{56,48},{64,56},{72,6... | collective-permute-start | bytes 38024 | tf_op jit(solution)/shard_map/ppermute | solution.py:17
  160.9 0.7 copy-start.1
where the time goes:
time: 162 us
  starting transfers between devices  66 us (41%)
  waiting for transfers between devices  44.8 us (28%)
  other arithmetic  22 us (14%)
  matrix products  16.2 us (10%)
  local copies, waits for them, and re-layouts  11.7 us (7%)
    all_to_all x2, starting transfers between devices, convnext_layer(): lax.all_to_all(pieces, 'lon', split_axis=0, concat_axis=0, tiled=True)  23.9 us
    all_to_all x2, waiting for transfers between devices, convnext_layer(): lax.all_to_all(spread, 'lon', split_axis=0, concat_axis=0, tiled=True)  23.7 us
    ppermute x4, starting transfers between devices, extended_2(): after = lax.ppermute(leading, axis, down)  22.4 us
    all_to_all x2, waiting for transfers between devices, convnext_layer(): lax.all_to_all(pieces, 'lon', split_axis=0, concat_axis=0, tiled=True)  18.7 us
    dot_general x4, matrix products, finish(): jnp.dot(w_reduce, hidden, preferred_element_type=jnp.float32)  16.2 us
    add x2, other arithmetic, depthwise(): summed + kernel[:, shift_row, shift_col, None, None] * band_rows[:, shift...  15.6 us
    ppermute x4, starting transfers between devices, extended_2(): before = lax.ppermute(last, axis, up)  10.5 us
    all_to_all x2, starting transfers between devices, convnext_layer(): lax.all_to_all(spread, 'lon', split_axis=0, concat_axis=0, tiled=True)  9.23 us
  transfers between devices with their start and end apart: 12, of which 6 were waited for; matrix products, arithmetic and copies ran while one was open for 5% of the time, Pallas kernels for 0%

commit v1 on v0

v1 whole, which is shorter than its diff:
```python
import functools

import jax
import jax.numpy as jnp
import numpy as np
from jax import lax
from jax.experimental import pallas as pl
from jax.experimental.pallas import tpu as pltpu
from jax.sharding import PartitionSpec as P

LAYERS = 2
C = 96
HID = 384
ROWS = 16
COLS = 128
GROUPS = C // 16
MESH = pl.DeviceIdType.MESH


def lane_ids(shape):
    return lax.broadcasted_iota(jnp.int32, shape, len(shape) - 1)


def build_weights(layer, vec, conv_w, colv):
    spread_shape = (COLS, 7 * COLS)
    tap = lax.broadcasted_iota(jnp.int32, spread_shape, 0)
    lane = lane_ids(spread_shape)
    rest = lane % COLS
    wanted = (rest // 16) * 7 + lane // COLS
    spread = jnp.where((tap == wanted) & (rest < 112), 1.0, 0.0).astype(jnp.bfloat16)
    taps = vec[layer].astype(jnp.bfloat16)
    flat = jnp.dot(taps, spread, preferred_element_type=jnp.float32)
    sub = lax.broadcasted_iota(jnp.int32, (C, COLS), 0)
    own = (lane_ids((C, COLS)) % 16) == (sub % 16)
    for d in range(7):
        band = jnp.where(own, flat[:, d * COLS : (d + 1) * COLS], 0.0)
        wide = jnp.concatenate([band, jnp.zeros_like(band)], axis=1)
        for r in range(10):
            moved = wide if r == 0 else pltpu.roll(wide, 16 * r, axis=1)
            moved = moved.astype(jnp.bfloat16)
            conv_w[layer, :, r * 16 : (r + 1) * 16, d * 256 : (d + 1) * 256] = moved.reshape(GROUPS, 16, 256)
    for k in range(4):
        colv[layer, k] = jnp.broadcast_to(vec[layer, :, 49 + k : 50 + k], (C, COLS))


def kernel(
    x_in, mask, vec, w_e, w_r, out,
    x_ext, pack, pack_l, pack_r, q_mid, q_up, q_down, mirror, q_mirror,
    conv_w, colv, shifted, mixed, send, recv,
):
    lat, lon = lax.axis_index("lat"), lax.axis_index("lon")
    nlat, nlon = lax.axis_size("lat"), lax.axis_size("lon")
    left = {"lat": lat, "lon": lax.rem(lon + nlon - 1, nlon)}
    right = {"lat": lat, "lon": lax.rem(lon + 1, nlon)}
    partner = {"lat": lat, "lon": nlon - 1 - lon}
    above = {"lat": jnp.minimum(lat + 1, nlat - 1), "lon": lon}
    below = {"lat": jnp.maximum(lat - 1, 0), "lon": lon}
    at_top = lat == nlat - 1
    not_top = lat < nlat - 1
    not_bottom = lat > 0
    barrier = pltpu.get_barrier_semaphore()

    def greet(device):
        pl.semaphore_signal(barrier, inc=1, device_id=device, device_id_type=MESH)

    greet(left)
    greet(right)
    pl.when(at_top)(lambda: greet(partner))
    pl.when(not_top)(lambda: greet(above))
    pl.when(not_bottom)(lambda: greet(below))

    lane = lane_ids((C, COLS))

    def fill_pack(layer):
        acc = pltpu.roll(x_ext[layer, 3], 3, axis=1)
        for r in range(1, ROWS):
            acc = jnp.where(lane // 8 == r, pltpu.roll(x_ext[layer, 3 + r], 8 * r + 3, axis=1), acc)
        pack[layer] = acc

    def fill_mirror(layer):
        rows = lax.broadcasted_iota(jnp.int32, (COLS, COLS), 0)
        flip = jnp.where(rows + lane_ids((COLS, COLS)) == COLS - 1, 1.0, 0.0).astype(jnp.bfloat16)
        for r in range(3):
            mirror[layer, r] = jnp.dot(
                x_ext[layer, 18 - r], flip, preferred_element_type=jnp.float32
            ).astype(jnp.bfloat16)

    def fill_q_mirror(layer):
        rows = lax.broadcasted_iota(jnp.int32, (COLS, COLS), 0)
        total = rows + lane_ids((COLS, COLS))
        flip = jnp.where((total == 125) | (total == 253), 1.0, 0.0).astype(jnp.bfloat16)
        q_mirror[layer] = jnp.dot(
            q_mid[layer], flip, preferred_element_type=jnp.float32
        ).astype(jnp.bfloat16)

    def remote(src, dst, slot, device):
        return pltpu.make_async_remote_copy(
            src_ref=src, dst_ref=dst, send_sem=send.at[slot], recv_sem=recv.at[slot],
            device_id=device, device_id_type=MESH,
        )

    def copy(layer, k):
        base = 8 * layer
        if k == 0:
            return remote(pack.at[layer], pack_r.at[layer], base, left)
        if k == 1:
            return remote(pack.at[layer], pack_l.at[layer], base + 1, right)
        if k == 2:
            return remote(x_ext.at[layer, pl.ds(3, 3)], x_ext.at[layer, pl.ds(19, 3)], base + 2, below)
        if k == 3:
            return remote(x_ext.at[layer, pl.ds(16, 3)], x_ext.at[layer, pl.ds(0, 3)], base + 3, above)
        if k == 4:
            return remote(q_mid.at[layer], q_up.at[layer], base + 4, below)
        if k == 5:
            return remote(q_mid.at[layer], q_down.at[layer], base + 5, above)
        if k == 6:
            return remote(mirror.at[layer], x_ext.at[layer, pl.ds(19, 3)], base + 6, partner)
        return remote(q_mirror.at[layer], q_up.at[layer], base + 7, partner)

    def send_first(layer):
        copy(layer, 0).start()
        copy(layer, 1).start()
        pl.when(not_bottom)(lambda: copy(layer, 2).start())
        pl.when(not_top)(lambda: copy(layer, 3).start())
        pl.when(at_top)(lambda: copy(layer, 6).start())

    def send_edges(layer):
        copy(layer, 0).wait_recv()
        copy(layer, 1).wait_recv()
        q_mid[layer] = jnp.where(lane % 8 >= 3, pack_r[layer], pack_l[layer])
        pl.when(not_bottom)(lambda: copy(layer, 4).start())
        pl.when(not_top)(lambda: copy(layer, 5).start())

        @pl.when(at_top)
        def _():
            fill_q_mirror(layer)
            copy(layer, 7).start()

    def wait_rows(layer):
        @pl.when(not_bottom)
        def _():
            copy(layer, 3).wait_recv()
            copy(layer, 5).wait_recv()

        @pl.when(lat == 0)
        def _():
            x_ext[layer, 0:3] = jnp.zeros((3, C, COLS), jnp.bfloat16)
            q_down[layer] = jnp.zeros((C, COLS), jnp.bfloat16)

        @pl.when(not_top)
        def _():
            copy(layer, 2).wait_recv()
            copy(layer, 4).wait_recv()

        @pl.when(at_top)
        def _():
            copy(layer, 6).wait_recv()
            copy(layer, 7).wait_recv()

    def wait_sends(layer):
        copy(layer, 0).wait_send()
        copy(layer, 1).wait_send()

        @pl.when(not_bottom)
        def _():
            copy(layer, 2).wait_send()
            copy(layer, 4).wait_send()

        @pl.when(not_top)
        def _():
            copy(layer, 3).wait_send()
            copy(layer, 5).wait_send()

        @pl.when(at_top)
        def _():
            copy(layer, 6).wait_send()
            copy(layer, 7).wait_send()

    def shift_row(layer, e, q, q_row):
        x = x_ext[layer, e]
        z = pltpu.roll(q, 2 * COLS - 3 - 8 * q_row, axis=1)
        for d in range(-3, 4):
            if d == 0:
                y = x
            else:
                outside = lane < d if d > 0 else lane >= COLS + d
                y = pltpu.roll(jnp.where(outside, z, x), (COLS - d) % COLS, axis=1)
            shifted[:, d + 3, e] = y.reshape(GROUPS, 16, COLS)

    def conv(layer, g, first, last, start):
        w = conv_w[layer, g, first * 16 : last * 16, :]
        x = shifted[g, :, start : start + 16].reshape(7 * 256, COLS)
        got = jnp.dot(w, x, preferred_element_type=jnp.float32)
        mixed[start + first : start + last, g] = got.reshape(last - first, 16, COLS)

    def two(v):
        return jnp.concatenate([v, v], axis=1)

    def mlp(layer, r0, r1):
        def both(pick):
            return jnp.concatenate([pick(r0), pick(r1)], axis=1)

        c = both(lambda r: mixed[r].reshape(C, COLS)) + two(colv[layer, 0])
        mean = jnp.sum(c, axis=0, keepdims=True) * (1.0 / C)
        c = c - mean
        var = jnp.sum(c * c, axis=0, keepdims=True) * (1.0 / C)
        n = c * lax.rsqrt(var + 1e-6) * two(colv[layer, 1]) + two(colv[layer, 2])
        ones = jnp.where(lax.broadcasted_iota(jnp.int32, (32, 2 * COLS), 0) < 2, 1.0, 0.0)
        n = jnp.concatenate([n, ones], axis=0).astype(jnp.bfloat16)
        h = jnp.dot(w_e[layer], n, preferred_element_type=jnp.float32)
        h = (0.5 * h * (1.0 + lax.erf(h * np.float32(np.sqrt(0.5))))).astype(jnp.bfloat16)
        u = jnp.dot(w_r[layer], h, preferred_element_type=jnp.float32) + two(colv[layer, 3])
        x = both(lambda r: x_ext[layer, 3 + r]).astype(jnp.float32)
        flags = both(lambda r: mask[pl.ds(r, 1), :]).astype(jnp.float32)
        y = (flags * (x + u)).astype(jnp.bfloat16)
        for k, r in enumerate((r0, r1)):
            part = y[:, k * COLS : (k + 1) * COLS]
            if layer == LAYERS - 1:
                out[r] = part
            else:
                x_ext[layer + 1, 3 + r] = part

    def loop(count, body):
        def step(i, carry):
            body(i)
            return carry

        lax.fori_loop(0, count, step, 0)

    def prepare(layer):
        fill_pack(layer)
        pl.when(at_top)(lambda: fill_mirror(layer))

    def spread_row(k):
        return k + 10 * ((k + 3) // 6)

    x_ext[0, 3:19] = x_in[...]
    prepare(0)
    pl.semaphore_wait(barrier, jnp.where(not_bottom, 4, 3))
    send_first(0)
    for layer in range(LAYERS):
        build_weights(layer, vec, conv_w, colv)
    for layer in range(LAYERS):
        if layer > 0:
            prepare(layer)
            send_first(layer)
        send_edges(layer)
        q = q_mid[layer]
        loop(ROWS, lambda r: shift_row(layer, r + 3, q, r))
        loop(GROUPS, lambda g: conv(layer, g, 0, 10, 3))
        loop(5, lambda k: mlp(layer, 2 * k + 3, 2 * k + 4))
        wait_rows(layer)
        for e in range(3):
            shift_row(layer, e, q_down[layer], 13 + e)
            shift_row(layer, 19 + e, q_up[layer], e)
        loop(GROUPS, lambda g: conv(layer, g, 0, 3, 0))
        loop(GROUPS, lambda g: conv(layer, g, 7, 10, 6))
        loop(3, lambda k: mlp(layer, spread_row(2 * k), spread_row(2 * k + 1)))
    for layer in range(LAYERS):
        wait_sends(layer)


def per_device(
    field, land_mask, depth_kernel, depth_bias, norm_gain, norm_bias, w_expand, b_expand, w_reduce, b_reduce
):
    x = jnp.transpose(field, (1, 0, 2))
    vec = jnp.concatenate(
        [depth_kernel.reshape(LAYERS, C, 49)]
        + [v[:, :, None] for v in (depth_bias, norm_gain, norm_bias, b_reduce)]
        + [jnp.zeros((LAYERS, C, COLS - 53), jnp.float32)],
        axis=2,
    )
    high = b_expand.astype(jnp.bfloat16)
    low = (b_expand - high.astype(jnp.float32)).astype(jnp.bfloat16)
    w_e = jnp.concatenate(
        [w_expand, high[:, :, None], low[:, :, None], jnp.zeros((LAYERS, HID, COLS - C - 2), jnp.bfloat16)], axis=2
    )
    tile = (LAYERS, C, COLS)
    bf = jnp.bfloat16
    vmem = pl.BlockSpec(memory_space=pltpu.VMEM)
    out = pl.pallas_call(
        kernel,
        out_shape=jax.ShapeDtypeStruct((ROWS, C, COLS), bf),
        in_specs=[vmem] * 5,
        out_specs=vmem,
        scratch_shapes=[
            pltpu.VMEM((LAYERS, ROWS + 6, C, COLS), bf),
            pltpu.VMEM(tile, bf),
            pltpu.VMEM(tile, bf),
            pltpu.VMEM(tile, bf),
            pltpu.VMEM(tile, bf),
            pltpu.VMEM(tile, bf),
            pltpu.VMEM(tile, bf),
            pltpu.VMEM((LAYERS, 3, C, COLS), bf),
            pltpu.VMEM(tile, bf),
            pltpu.VMEM((LAYERS, GROUPS, 160, 7 * 256), bf),
            pltpu.VMEM((LAYERS, 4, C, COLS), jnp.float32),
            pltpu.VMEM((GROUPS, 7, ROWS + 6, 16, COLS), bf),
            pltpu.VMEM((ROWS, GROUPS, 16, COLS), jnp.float32),
            pltpu.SemaphoreType.DMA((16,)),
            pltpu.SemaphoreType.DMA((16,)),
        ],
        compiler_params=pltpu.CompilerParams(
            collective_id=0, has_side_effects=True, vmem_limit_bytes=48 * 1024 * 1024
        ),
    )(x, land_mask, vec, w_e, w_reduce)
    return jnp.transpose(out, (1, 0, 2))


def solution(mesh):
    placed = (P(None, "lat", "lon"), P("lat", "lon"), P(), P(), P(), P(), P(), P(), P(), P())
    return jax.shard_map(
        per_device, mesh=mesh, in_specs=placed, out_specs=P(None, "lat", "lon"), check_vma=False
    )
```

time: 162 us -> 53 us (0.33)
  starting transfers between devices: 66 us -> 0 us
  waiting for transfers between devices: 44.8 us -> 0 us
  Pallas kernels: 0 us -> 44.3 us
  other arithmetic: 22 us -> 0.2 us
  matrix products: 16.2 us -> 0 us
  local copies, waits for them, and re-layouts: 11.7 us -> 7.79 us
    pallas_call x0 -> x1, Pallas kernels: none -> 44.3 us  [per_device(): pl.pallas_call(kernel, out_shape=jax.ShapeDtypeStruct((ROWS, C, COLS), bf...]
    all_to_all x4 -> x0, waiting for transfers between devices: 42.4 us -> none  [the longest x2 23.7 us: convnext_layer(): lax.all_to_all(spread, 'lon', split_axis=0, concat_axis=0, tiled=True)]
    all_to_all x4 -> x0, starting transfers between devices: 33.1 us -> none  [the longest x2 23.9 us: convnext_layer(): lax.all_to_all(pieces, 'lon', split_axis=0, concat_axis=0, tiled=True)]
    ppermute x8 -> x0, starting transfers between devices: 32.9 us -> none  [the longest x4 22.4 us: extended_2(): after = lax.ppermute(leading, axis, down)]
    dot_general x4 -> x0, matrix products: 16.2 us -> none  [finish(): jnp.dot(w_reduce, hidden, preferred_element_type=jnp.float32)]
    add x2 -> x0, other arithmetic: 15.6 us -> none  [depthwise(): summed + kernel[:, shift_row, shift_col, None, None] * band_rows[:, shift...]
    all_to_all x6 -> x0, other arithmetic: 4.26 us -> none  [the longest x4 2.16 us: convnext_layer(): lax.all_to_all(spread, 'lon', split_axis=0, concat_axis=0, tiled=True)]
    ppermute x8 -> x0, waiting for transfers between devices: 2.39 us -> none  [the longest x4 2.38 us: extended_2(): after = lax.ppermute(leading, axis, down)]
  transfers between devices with their start and end apart: 12 -> 0, of which waited for: 6 -> 0; matrix products, arithmetic and copies ran while one was open for 5% -> 0% of each run, Pallas kernels for 0% -> 0%
where the time goes in v1:
time: 53 us; the launch traced here: 52.4 us
  Pallas kernels  44.3 us (84%)
  local copies, waits for them, and re-layouts  7.79 us (15%)
    pallas_call x1, Pallas kernels, per_device(): pl.pallas_call(kernel, out_shape=jax.ShapeDtypeStruct((ROWS, C, COLS), bf...  44.3 us
    unnamed x20, local copies, waits for them, and re-layouts  4.85 us

profile of v1, /device:TPU:6, one launch (start us, length us, event | category | flops | bytes accessed | tf_op | source)
XLA Modules:
  0.0 52.4 jit_solution(4991877092925348090)
XLA Ops:
  0.0 0.0 copy-start.4
  0.0 0.1 pad.3.clone
  0.1 0.6 %copy-done.4 = f32[2,384]{1,0:T(2,128)S(1)} copy-done((f32[2,384]{1,0:T(2,128)S(1)}, f32[2,384]{1,0:T(2,128)}, u32[]{:S(2)}) %copy-start.4) | copy-done | bytes 3096
  0.7 0.0 copy-start.5
  0.7 0.9 %copy.26 = f32[2,96,49]{2,1,0:T(8,128)S(1)} copy(f32[2,96,49]{1,0,2:T(2,128)} %bitcast.15) | data formatting | bytes 75264 | tf_op jit(solution)/shard_map/reshape | solution.py:268
  1.6 0.0 copy-done.5
  1.6 0.0 copy-start.6
  1.6 0.1 copy.27
  1.7 0.5 %copy-done.6 = f32[2,96]{1,0:T(2,128)S(1)} copy-done((f32[2,96]{1,0:T(2,128)S(1)}, f32[2,96]{1,0:T(2,128)}, u32[]{:S(2)}) %copy-start.6) | copy-done | bytes 792
  2.3 0.0 copy-start.7
  2.3 0.1 copy.28
  2.4 0.6 %copy-done.7 = f32[2,96]{1,0:T(2,128)S(1)} copy-done((f32[2,96]{1,0:T(2,128)S(1)}, f32[2,96]{1,0:T(2,128)}, u32[]{:S(2)}) %copy-start.7) | copy-done | bytes 792
  3.0 0.0 copy-start.8
  3.0 0.1 copy.29
  3.1 0.6 %copy-done.8 = f32[2,96]{1,0:T(2,128)S(1)} copy-done((f32[2,96]{1,0:T(2,128)S(1)}, f32[2,96]{1,0:T(2,128)}, u32[]{:S(2)}) %copy-start.8) | copy-done | bytes 792
  3.6 0.1 copy.30
  3.8 0.2 concatenate.6.vec
  4.0 0.2 copy.32
  4.2 0.0 copy-start.3
  4.2 0.2 copy.33
  4.4 0.7 %copy-done.3 = bf16[2,384,96]{1,2,0:T(8,128)(2,1)S(1)} copy-done((bf16[2,384,96]{1,2,0:T(8,128)(2,1)S(1)}, bf16[2,384,96]{1,2,0:T(8,128)(2,1)}, u32[]{:S(2)}) %copy-start.3) | copy-done | bytes 147480
  5.1 0.2 copy.31
  5.3 0.0 copy-start.2
  5.3 0.2 maximum_maximum_fusion.w_e
  5.5 0.8 %copy-done.2 = bf16[96,16,128]{2,1,0:T(8,128)(2,1)S(1)} copy-done((bf16[96,16,128]{2,1,0:T(8,128)(2,1)S(1)}, bf16[96,16,128]{2,1,0:T(8,128)(2,1)}, u32[]{:S(2)}) %copy-start.2) | copy-done | bytes 393240
  6.3 0.0 copy-start
  6.3 0.0 copy-start.1
  6.3 0.1 copy.36
  6.4 0.8 %copy-done = bf16[2,96,384]{2,1,0:T(8,128)(2,1)S(1)} copy-done((bf16[2,96,384]{2,1,0:T(8,128)(2,1)S(1)}, bf16[2,96,384]{2,1,0:T(8,128)(2,1)}, u32[]{:S(2)}) %copy-start) | copy-done | bytes 147480
  7.2 0.0 copy-done.1
  7.2 44.3 %shard_map.100 = bf16[16,96,128]{2,1,0:T(8,128)(2,1)S(1)} custom-call(bf16[16,96,128]{2,1,0:T(8,128)(2,1)S(1)} %bitcast.14, s32[16,128]{1,0:T(8,128)S(1)} %copy-done.1, f32[2,96,128]{2,1,0:T(8,128)S(1)} %concatenate.6.vec, bf16[2,384,128]{2,1,0:T(8,128)(2,1)S(1)} %maximum_maximum_fusion.w_e, bf16[2,96,384]{2,1,0:T(8,128)(2,1)S(1)} %copy-done), custom_call_target="tpu_custom_call" | custom-call | tf_op jit(solution)/shard_map/pallas_call | solution.py:281
  51.5 0.9 %copy.34 = bf16[96,16,128]{2,1,0:T(8,128)(2,1)} copy(bf16[96,16,128]{2,0,1:T(8,128)(2,1)S(1)} %bitcast.13) | data formatting | bytes 786432 | tf_op jit(solution)/shard_map/transpose | solution.py:307
  (3 shorter events, 0.0 us)
Async XLA Ops:
  0.0 0.7 %copy-start.4 = (f32[2,384]{1,0:T(2,128)S(1)}, f32[2,384]{1,0:T(2,128)}, u32[]{:S(2)}) copy-start(f32[2,384]{1,0:T(2,128)} %param.17) | copy-start | bytes 9220
  0.7 0.9 %copy-start.5 = (f32[2,96]{1,0:T(2,128)S(1)}, f32[2,96]{1,0:T(2,128)}, u32[]{:S(2)}) copy-start(f32[2,96]{1,0:T(2,128)} %param.13) | copy-start | bytes 2308
  1.6 0.7 %copy-start.6 = (f32[2,96]{1,0:T(2,128)S(1)}, f32[2,96]{1,0:T(2,128)}, u32[]{:S(2)}) copy-start(f32[2,96]{1,0:T(2,128)} %param.14) | copy-start | bytes 2308
  2.3 0.7 %copy-start.7 = (f32[2,96]{1,0:T(2,128)S(1)}, f32[2,96]{1,0:T(2,128)}, u32[]{:S(2)}) copy-start(f32[2,96]{1,0:T(2,128)} %param.15) | copy-start | bytes 2308
  3.0 0.7 %copy-start.8 = (f32[2,96]{1,0:T(2,128)S(1)}, f32[2,96]{1,0:T(2,128)}, u32[]{:S(2)}) copy-start(f32[2,96]{1,0:T(2,128)} %param.19) | copy-start | bytes 2308
  4.2 0.9 %copy-start.3 = (bf16[2,384,96]{1,2,0:T(8,128)(2,1)S(1)}, bf16[2,384,96]{1,2,0:T(8,128)(2,1)}, u32[]{:S(2)}) copy-start(bf16[2,384,96]{1,2,0:T(8,128)(2,1)} %param.16) | copy-start | bytes 442372
  5.3 1.0 %copy-start.2 = (bf16[96,16,128]{2,1,0:T(8,128)(2,1)S(1)}, bf16[96,16,128]{2,1,0:T(8,128)(2,1)}, u32[]{:S(2)}) copy-start(bf16[96,16,128]{2,1,0:T(8,128)(2,1)} %param.10) | copy-start | bytes 1179652
  6.3 0.9 %copy-start = (bf16[2,96,384]{2,1,0:T(8,128)(2,1)S(1)}, bf16[2,96,384]{2,1,0:T(8,128)(2,1)}, u32[]{:S(2)}) copy-start(bf16[2,96,384]{2,1,0:T(8,128)(2,1)} %w_r.1) | copy-start | bytes 442372
  6.3 0.9 %copy-start.1 = (s32[16,128]{1,0:T(8,128)S(1)}, s32[16,128]{1,0:T(8,128)}, u32[]{:S(2)}) copy-start(s32[16,128]{1,0:T(8,128)} %mask.1) | copy-start | bytes 24580

commit v2 on v1

v2 whole, which is shorter than its diff:
```python
import jax
import jax.numpy as jnp
import numpy as np
from jax import lax
from jax.experimental import pallas as pl
from jax.experimental.pallas import tpu as pltpu
from jax.sharding import PartitionSpec as P

LAYERS = 2
C = 96
HID = 384
ROWS = 16
COLS = 128
GROUPS = C // 16
MESH = pl.DeviceIdType.MESH
BF = jnp.bfloat16
F32 = jnp.float32
SIDE = (0, 1, 2, 4, 5, 6)


def ids(shape, dim):
    return lax.broadcasted_iota(jnp.int32, shape, dim)


def kernel(
    field, mask_in, taps_in, dbias_in, gain_in, nbias_in, w_e_in, b_e_in, w_r_in, b_r_in, out,
    raw, mask, taps, dbias, gain, nbias, w_e_raw, b_e, w_r, b_r,
    cells, x_ext, pack, pack_l, pack_r, q_mid, q_up, q_down, mirror, q_mirror,
    table, w_e, conv_w, low_w, high_w, side_w, colv, shifted, mixed, edge, load, send, recv,
):
    lat, lon = lax.axis_index("lat"), lax.axis_index("lon")
    nlat, nlon = lax.axis_size("lat"), lax.axis_size("lon")
    left = {"lat": lat, "lon": lax.rem(lon + nlon - 1, nlon)}
    right = {"lat": lat, "lon": lax.rem(lon + 1, nlon)}
    partner = {"lat": lat, "lon": nlon - 1 - lon}
    above = {"lat": jnp.minimum(lat + 1, nlat - 1), "lon": lon}
    below = {"lat": jnp.maximum(lat - 1, 0), "lon": lon}
    at_top = lat == nlat - 1
    not_top = lat < nlat - 1
    not_bottom = lat > 0
    barrier = pltpu.get_barrier_semaphore()

    def greet(device):
        pl.semaphore_signal(barrier, inc=1, device_id=device, device_id_type=MESH)

    greet(left)
    greet(right)
    pl.when(at_top)(lambda: greet(partner))
    pl.when(not_top)(lambda: greet(above))
    pl.when(not_bottom)(lambda: greet(below))

    pairs = (
        (field, raw), (taps_in, taps), (dbias_in, dbias), (gain_in, gain), (nbias_in, nbias), (b_r_in, b_r),
        (w_e_in, w_e_raw), (b_e_in, b_e), (w_r_in, w_r), (mask_in, mask),
    )
    loads = [pltpu.make_async_copy(src, dst, load.at[k]) for k, (src, dst) in enumerate(pairs)]
    for one in loads:
        one.start()

    def remote(src, dst, slot, device):
        return pltpu.make_async_remote_copy(
            src_ref=src, dst_ref=dst, send_sem=send.at[slot], recv_sem=recv.at[slot],
            device_id=device, device_id_type=MESH,
        )

    def copy(layer, k):
        base = 8 * layer
        if k == 0:
            return remote(pack.at[layer], pack_r.at[layer], base, left)
        if k == 1:
            return remote(pack.at[layer], pack_l.at[layer], base + 1, right)
        if k == 2:
            return remote(x_ext.at[layer, pl.ds(3, 3)], x_ext.at[layer, pl.ds(19, 3)], base + 2, below)
        if k == 3:
            return remote(x_ext.at[layer, pl.ds(16, 3)], x_ext.at[layer, pl.ds(0, 3)], base + 3, above)
        if k == 4:
            return remote(q_mid.at[layer], q_up.at[layer], base + 4, below)
        if k == 5:
            return remote(q_mid.at[layer], q_down.at[layer], base + 5, above)
        if k == 6:
            return remote(mirror.at[layer], x_ext.at[layer, pl.ds(19, 3)], base + 6, partner)
        return remote(q_mirror.at[layer], q_up.at[layer], base + 7, partner)

    lane = ids((C, COLS), 1)

    def loop(count, body, unroll=1):
        def step(i, carry):
            body(i)
            return carry

        lax.fori_loop(0, count, step, 0, unroll=unroll)

    def flipped(value, total):
        away = (ids((COLS, COLS), 0) + ids((COLS, COLS), 1)) % COLS
        flip = jnp.where(away == total, 1.0, 0.0).astype(BF)
        return jnp.dot(value, flip, preferred_element_type=F32).astype(BF)

    def fill_pack(layer):
        acc = pltpu.roll(x_ext[layer, 3], 3, axis=1)
        for r in range(1, ROWS):
            acc = jnp.where(lane // 8 == r, pltpu.roll(x_ext[layer, 3 + r], 8 * r + 3, axis=1), acc)
        pack[layer] = acc

    def fill_mirror(layer):
        for r in range(3):
            mirror[layer, r] = flipped(x_ext[layer, 18 - r], COLS - 1)

    def send_strips(layer):
        pl.when(not_bottom)(lambda: copy(layer, 2).start())
        pl.when(not_top)(lambda: copy(layer, 3).start())

        @pl.when(at_top)
        def _():
            fill_mirror(layer)
            copy(layer, 6).start()

    def send_pack(layer):
        fill_pack(layer)
        copy(layer, 0).start()
        copy(layer, 1).start()

    def send_edges(layer):
        copy(layer, 0).wait_recv()
        copy(layer, 1).wait_recv()
        q_mid[layer] = jnp.where(lane % 8 >= 3, pack_r[layer], pack_l[layer])
        pl.when(not_bottom)(lambda: copy(layer, 4).start())
        pl.when(not_top)(lambda: copy(layer, 5).start())

        @pl.when(at_top)
        def _():
            q_mirror[layer] = flipped(q_mid[layer], 125)
            copy(layer, 7).start()

    def wait_rows(layer):
        @pl.when(not_bottom)
        def _():
            copy(layer, 3).wait_recv()
            copy(layer, 5).wait_recv()

        @pl.when(lat == 0)
        def _():
            x_ext[layer, 0:3] = jnp.zeros((3, C, COLS), BF)
            q_down[layer] = jnp.zeros((C, COLS), BF)

        @pl.when(not_top)
        def _():
            copy(layer, 2).wait_recv()
            copy(layer, 4).wait_recv()

        @pl.when(at_top)
        def _():
            copy(layer, 6).wait_recv()
            copy(layer, 7).wait_recv()

    def wait_sends(layer):
        copy(layer, 0).wait_send()
        copy(layer, 1).wait_send()

        @pl.when(not_bottom)
        def _():
            copy(layer, 2).wait_send()
            copy(layer, 4).wait_send()

        @pl.when(not_top)
        def _():
            copy(layer, 3).wait_send()
            copy(layer, 5).wait_send()

        @pl.when(at_top)
        def _():
            copy(layer, 6).wait_send()
            copy(layer, 7).wait_send()

    def build_weights(layer):
        table[...] = jnp.zeros((COLS, COLS), F32)
        table[0:49, 0:C] = taps[:, layer, :]
        for k, v in enumerate((dbias, gain, nbias, b_r)):
            table[49 + k : 50 + k, 0:C] = v[layer : layer + 1, :]
        vec = jnp.transpose(table[...])[0:C]
        for k in range(4):
            colv[layer, k] = jnp.broadcast_to(vec[:, 49 + k : 50 + k], (C, COLS))
        vec = vec.astype(BF)
        bias = b_e[layer : layer + 1, :]
        high = bias.astype(BF).astype(F32)
        wide = jnp.concatenate(
            [w_e_raw[layer].astype(F32), high, bias - high, jnp.zeros((COLS - C - 2, HID), F32)], axis=0
        )
        w_e[layer] = (0.5 * jnp.transpose(wide)).astype(BF)
        shape = (COLS, 7 * COLS)
        at = ids(shape, 1)
        rest = at % COLS
        spread = jnp.where((ids(shape, 0) == (rest // 16) * 7 + at // COLS) & (rest < 112), 1.0, 0.0).astype(BF)
        flat = jnp.dot(vec, spread, preferred_element_type=F32)
        own = (lane % 16) == (ids((C, COLS), 0) % 16)
        for d in range(7):
            band = jnp.where(own, flat[:, d * COLS : (d + 1) * COLS], 0.0)
            none = jnp.zeros_like(band)
            for r in range(ROWS):
                by = 16 * (r - 3)
                turned = band if by % COLS == 0 else pltpu.roll(band, by % COLS, axis=1)
                if by < 0:
                    low, high = jnp.where(lane < COLS + by, turned, 0.0), none
                elif by < COLS:
                    low, high = jnp.where(lane >= by, turned, 0.0), jnp.where(lane < by, turned, 0.0)
                else:
                    low, high = none, jnp.where(lane >= by - COLS, turned, 0.0)
                at_rows = slice(r * 16, (r + 1) * 16)
                conv_w[layer, :, at_rows, d * 256 : d * 256 + 128] = low.astype(BF).reshape(GROUPS, 16, COLS)
                conv_w[layer, :, at_rows, d * 256 + 128 : d * 256 + 256] = high.astype(BF).reshape(GROUPS, 16, COLS)
            for r in range(3):
                at_rows = slice(r * 16, (r + 1) * 16)
                turned = band if r == 0 else pltpu.roll(band, 16 * r, axis=1)
                part = jnp.where((lane >= 16 * r) & (lane < 48), turned, 0.0)
                low_w[layer, :, at_rows, d * 128 : d * 128 + 128] = part.astype(BF).reshape(GROUPS, 16, COLS)
                turned = band if r == 1 else pltpu.roll(band, (16 * r - 16) % COLS, axis=1)
                part = jnp.where((lane >= 80) & (lane < (112 if r == 0 else COLS)), turned, 0.0)
                high_w[layer, :, at_rows, d * 128 : d * 128 + 128] = part.astype(BF).reshape(GROUPS, 16, COLS)
        for k, d in enumerate(SIDE):
            shape = (COLS, 7 * COLS)
            at = ids(shape, 1)
            to = at % 8
            start = to + d - 3
            if d > 3:
                reach = (to < 3) & (start >= 3) & (start < 6)
            else:
                reach = (to >= 3) & (to < 6) & (start >= 0) & (start < 3)
            pick = jnp.where((ids(shape, 0) == (at // COLS) * 7 + d) & reach, 1.0, 0.0).astype(BF)
            got = jnp.dot(vec, pick, preferred_element_type=F32)
            for a in range(7):
                side_w[layer, k * 7 + a] = got[:, a * COLS : (a + 1) * COLS]

    def shift_own(layer, r):
        x = x_ext[layer, 3 + r]
        for d in range(-3, 4):
            y = x if d == 0 else pltpu.roll(x, (COLS - d) % COLS, axis=1)
            shifted[:, d + 3, 3 + r] = y.reshape(GROUPS, 16, COLS)

    def shift_halo(layer, e, q, q_row):
        x = x_ext[layer, e]
        z = pltpu.roll(q, 2 * COLS - 3 - 8 * q_row, axis=1)
        for d in range(-3, 4):
            if d == 0:
                y = x
            else:
                outside = lane < d if d > 0 else lane >= COLS + d
                y = pltpu.roll(jnp.where(outside, z, x), (COLS - d) % COLS, axis=1)
            shifted[:, d + 3, e] = y.reshape(GROUPS, 16, COLS)

    def conv_own(layer, g):
        x = shifted[g, :, 3:19].reshape(7 * 256, COLS)
        got = jnp.dot(conv_w[layer, g], x, preferred_element_type=F32)
        mixed[:, g] = got.reshape(ROWS, 16, COLS)

    def conv_halo(layer, g):
        x = shifted[g, :, 0:8].reshape(7 * 128, COLS)
        got = jnp.dot(low_w[layer, g], x, preferred_element_type=F32)
        mixed[0:3, g] += got.reshape(3, 16, COLS)
        x = shifted[g, :, 14:22].reshape(7 * 128, COLS)
        got = jnp.dot(high_w[layer, g], x, preferred_element_type=F32)
        mixed[13:16, g] += got.reshape(3, 16, COLS)

    def fill_edge(layer):
        delta = q_mid[layer].astype(F32) - pack[layer].astype(F32)
        total = jnp.zeros((C, COLS), F32)
        for a in range(7):
            by = 8 * (a - 3)
            if by > 0:
                rows = jnp.where(lane < by, 0.0, delta)
            elif by < 0:
                rows = jnp.where(lane >= COLS + by, 0.0, delta)
            else:
                rows = delta
            for k, d in enumerate(SIDE):
                total += side_w[layer, k * 7 + a] * pltpu.roll(rows, (3 * COLS - by - (d - 3)) % COLS, axis=1)
        edge[...] = total

    def two(v):
        return jnp.concatenate([v, v], axis=1)

    def mlp(layer, r0, r1):
        def both(pick):
            return jnp.concatenate([pick(r0), pick(r1)], axis=1)

        def rows(r):
            beside = pltpu.roll(edge[...], 2 * COLS - 3 - 8 * r, axis=1)
            return mixed[r].reshape(C, COLS) + jnp.where((lane < 3) | (lane >= COLS - 3), beside, 0.0)

        c = both(rows) + two(colv[layer, 0])
        mean = jnp.sum(c, axis=0, keepdims=True) * (1.0 / C)
        c = c - mean
        var = jnp.sum(c * c, axis=0, keepdims=True) * (1.0 / C)
        n = c * lax.rsqrt(var + 1e-6) * two(colv[layer, 1]) + two(colv[layer, 2])
        ones = jnp.where(ids((32, 2 * COLS), 0) < 2, 1.0, 0.0)
        n = jnp.concatenate([n, ones], axis=0).astype(BF)
        half = jnp.dot(w_e[layer], n, preferred_element_type=F32)
        h = (half + half * lax.erf(half * np.float32(np.sqrt(2.0)))).astype(BF)
        u = jnp.dot(w_r[layer], h, preferred_element_type=F32) + two(colv[layer, 3])
        x = both(lambda r: x_ext[layer, 3 + r]).astype(F32)
        flags = both(lambda r: mask[pl.ds(r, 1), :]).astype(F32)
        y = flags * (x + u)
        for k, r in enumerate((r0, r1)):
            part = y[:, k * COLS : (k + 1) * COLS]
            if layer == LAYERS - 1:
                cells[pl.ds(r, C, stride=ROWS), :] = part
            else:
                x_ext[layer + 1, 3 + r] = part.astype(BF)

    def spread_row(k):
        return k + 10 * ((k + 3) // 6)

    loads[0].wait()
    cells[...] = raw[...].astype(F32).reshape(C * ROWS, COLS)
    for r in range(ROWS):
        x_ext[0, 3 + r] = cells[pl.ds(r, C, stride=ROWS), :].astype(BF)
    fill_pack(0)
    pl.semaphore_wait(barrier, jnp.where(not_bottom, 4, 3))
    copy(0, 0).start()
    copy(0, 1).start()
    send_strips(0)
    for one in loads[1:]:
        one.wait()
    for layer in range(LAYERS):
        build_weights(layer)
    for layer in range(LAYERS):
        if layer > 0:
            send_strips(layer)
            send_pack(layer)
        loop(ROWS, lambda r: shift_own(layer, r), 4)
        send_edges(layer)
        loop(GROUPS, lambda g: conv_own(layer, g), 6)
        fill_edge(layer)
        loop(5, lambda k: mlp(layer, 2 * k + 3, 2 * k + 4), 5)
        wait_rows(layer)
        for e in range(3):
            shift_halo(layer, e, q_down[layer], 13 + e)
            shift_halo(layer, 19 + e, q_up[layer], e)
        loop(GROUPS, lambda g: conv_halo(layer, g), 6)
        loop(3, lambda k: mlp(layer, spread_row(2 * k), spread_row(2 * k + 1)), 3)
    out[...] = cells[...].reshape(C, ROWS, COLS).astype(BF)
    for layer in range(LAYERS):
        wait_sends(layer)


def per_device(
    field, land_mask, depth_kernel, depth_bias, norm_gain, norm_bias, w_expand, b_expand, w_reduce, b_reduce
):
    taps = jnp.transpose(depth_kernel, (2, 3, 0, 1)).reshape(49, LAYERS, C)
    args = (
        field, land_mask, taps, depth_bias, norm_gain, norm_bias, jnp.transpose(w_expand, (0, 2, 1)), b_expand,
        w_reduce, b_reduce,
    )
    tile = (LAYERS, C, COLS)
    held = [pltpu.VMEM(a.shape, a.dtype) for a in args]
    scratch = held + [
        pltpu.VMEM((C * ROWS, COLS), F32),
        pltpu.VMEM((LAYERS, ROWS + 6, C, COLS), BF),
    ]
    scratch += [pltpu.VMEM(tile, BF)] * 6
    scratch += [
        pltpu.VMEM((LAYERS, 3, C, COLS), BF),
        pltpu.VMEM(tile, BF),
        pltpu.VMEM((COLS, COLS), F32),
        pltpu.VMEM((LAYERS, HID, COLS), BF),
        pltpu.VMEM((LAYERS, GROUPS, 256, 7 * 256), BF),
        pltpu.VMEM((LAYERS, GROUPS, 48, 7 * 128), BF),
        pltpu.VMEM((LAYERS, GROUPS, 48, 7 * 128), BF),
        pltpu.VMEM((LAYERS, 42, C, COLS), F32),
        pltpu.VMEM((LAYERS, 4, C, COLS), F32),
        pltpu.VMEM((GROUPS, 7, ROWS + 6, 16, COLS), BF),
        pltpu.VMEM((ROWS, GROUPS, 16, COLS), F32),
        pltpu.VMEM((C, COLS), F32),
        pltpu.SemaphoreType.DMA((len(args),)),
        pltpu.SemaphoreType.DMA((16,)),
        pltpu.SemaphoreType.DMA((16,)),
    ]
    return pl.pallas_call(
        kernel,
        out_shape=jax.ShapeDtypeStruct((C, ROWS, COLS), BF),
        in_specs=[pl.BlockSpec(memory_space=pl.ANY)] * len(args),
        out_specs=pl.BlockSpec(memory_space=pltpu.VMEM),
        scratch_shapes=scratch,
        compiler_params=pltpu.CompilerParams(
            collective_id=0, has_side_effects=True, vmem_limit_bytes=56 * 1024 * 1024
        ),
    )(*args)


def solution(mesh):
    placed = (P(None, "lat", "lon"), P("lat", "lon"), P(), P(), P(), P(), P(), P(), P(), P())
    return jax.shard_map(
        per_device, mesh=mesh, in_specs=placed, out_specs=P(None, "lat", "lon"), check_vma=False
    )
```

time: 53 us -> 39.2 us (0.74)
  the two profiles are of different devices: /device:TPU:6 before, /device:TPU:70 now
where the time goes in v2:
time: 39.2 us; the launch traced here: 39 us
  Pallas kernels  37.3 us (95%)
  local copies, waits for them, and re-layouts  1.77 us (5%)
    pallas_call x1, Pallas kernels, per_device(): pl.pallas_call(kernel, out_shape=jax.ShapeDtypeStruct((C, ROWS, COLS), BF...  37.3 us
    unnamed x1, local copies, waits for them, and re-layouts  1.77 us

profile of v2, /device:TPU:70, one launch (start us, length us, event | category | flops | bytes accessed | tf_op | source)
XLA Modules:
  0.0 39.0 jit_solution(15901726527534683689)
XLA Ops:
  0.0 37.3 %shard_map.100 = bf16[96,16,128]{2,1,0:T(8,128)(2,1)} custom-call(bf16[96,16,128]{2,1,0:T(8,128)(2,1)} %field.1, s32[16,128]{1,0:T(8,128)} %mask_in.1, f32[49,2,96]{2,1,0:T(2,128)} %bitcast.5, f32[2,96]{1,0:T(2,128)} %dbias_in.1, f32[2,96]{1,0:T(2,128)} %gain_in.1, f32[2,96]{1,0:T(2,128)} %nbias_in.1, bf16[2,96,384]{2,1,0:T(8,128)(2,1)} %bitcast.4, ...), custom_call_target="tpu_custom_call" | custom-call | tf_op jit(solution)/shard_map/pallas_call | solution.py:376
  37.3 1.8 %copy.12 = bf16[96,16,128]{2,1,0:T(8,128)(2,1)} copy(bf16[96,16,128]{2,1,0:T(8,128)(2,1)} %shard_map.100) | data formatting | bytes 786432

commit v3 on v2

v3 whole, which is shorter than its diff:
```python
import jax
import jax.numpy as jnp
import numpy as np
from jax import lax
from jax.experimental import pallas as pl
from jax.experimental.pallas import tpu as pltpu
from jax.sharding import PartitionSpec as P

LAYERS = 2
C = 96
HID = 384
ROWS = 16
COLS = 128
GROUPS = C // 16
MESH = pl.DeviceIdType.MESH
BF = jnp.bfloat16
F32 = jnp.float32
SIDE = (0, 1, 2, 4, 5, 6)


def ids(shape, dim):
    return lax.broadcasted_iota(jnp.int32, shape, dim)


def kernel(
    field, mask_in, taps_in, dbias_in, gain_in, nbias_in, w_e_in, b_e_in, w_r_in, b_r_in, out,
    raw, mask, taps, dbias, gain, nbias, w_e_raw, b_e, w_r, b_r,
    cells, x_ext, pack, pack_l, pack_r, q_mid, q_halo, mirror, corner, corner_m, halo_t,
    table, w_e, conv_w, low_w, high_w, side_w, colv, shifted, mixed, edge, load, send, recv,
):
    lat, lon = lax.axis_index("lat"), lax.axis_index("lon")
    nlat, nlon = lax.axis_size("lat"), lax.axis_size("lon")
    lon_l, lon_r = lax.rem(lon + nlon - 1, nlon), lax.rem(lon + 1, nlon)
    lat_u, lat_d = jnp.minimum(lat + 1, nlat - 1), jnp.maximum(lat - 1, 0)
    fold_r, fold_l = lax.rem(2 * nlon - 2 - lon, nlon), lax.rem(nlon - lon, nlon)
    at_top = lat == nlat - 1
    not_top = lat < nlat - 1
    not_bottom = lat > 0
    fold_r_away = at_top & (fold_r != lon)
    fold_l_away = at_top & (fold_l != lon)
    left = {"lat": lat, "lon": lon_l}
    right = {"lat": lat, "lon": lon_r}
    peers = (
        (left, None), (right, None),
        ({"lat": lat_d, "lon": lon}, not_bottom),
        ({"lat": lat_d, "lon": lon_l}, not_bottom),
        ({"lat": lat_d, "lon": lon_r}, not_bottom),
        ({"lat": lat_u, "lon": lon}, not_top),
        ({"lat": lat_u, "lon": lon_l}, not_top),
        ({"lat": lat_u, "lon": lon_r}, not_top),
        ({"lat": lat, "lon": nlon - 1 - lon}, at_top),
        ({"lat": lat, "lon": fold_r}, fold_r_away),
        ({"lat": lat, "lon": fold_l}, fold_l_away),
    )
    barrier = pltpu.get_barrier_semaphore()

    def when(condition, body):
        if condition is None:
            body()
        else:
            pl.when(condition)(body)

    for device, condition in peers:
        when(
            condition,
            lambda: pl.semaphore_signal(barrier, inc=1, device_id=device, device_id_type=MESH),
        )
    n_peers = sum(1 if c is None else c.astype(jnp.int32) for _, c in peers)

    pairs = (
        (field, raw), (taps_in, taps), (dbias_in, dbias), (gain_in, gain), (nbias_in, nbias), (b_r_in, b_r),
        (w_e_in, w_e_raw), (b_e_in, b_e), (w_r_in, w_r), (mask_in, mask),
    )
    loads = [pltpu.make_async_copy(src, dst, load.at[k]) for k, (src, dst) in enumerate(pairs)]
    for one in loads:
        one.start()

    def remote(src, dst, slot, device):
        return pltpu.make_async_remote_copy(
            src_ref=src, dst_ref=dst, send_sem=send.at[slot], recv_sem=recv.at[slot],
            device_id=device, device_id_type=MESH,
        )

    def copy(layer, k):
        src, dst = (
            (pack.at[layer], pack_r.at[layer]),
            (pack.at[layer], pack_l.at[layer]),
            (x_ext.at[layer, pl.ds(3, 3)], x_ext.at[layer, pl.ds(19, 3)]),
            (corner.at[layer, pl.ds(0, 32)], halo_t.at[layer, 1, pl.ds(0, 32)]),
            (corner.at[layer, pl.ds(0, 32)], halo_t.at[layer, 0, pl.ds(0, 32)]),
            (x_ext.at[layer, pl.ds(16, 3)], x_ext.at[layer, pl.ds(0, 3)]),
            (corner.at[layer, pl.ds(96, 32)], halo_t.at[layer, 1, pl.ds(96, 32)]),
            (corner.at[layer, pl.ds(96, 32)], halo_t.at[layer, 0, pl.ds(96, 32)]),
            (mirror.at[layer], x_ext.at[layer, pl.ds(19, 3)]),
            (corner_m.at[layer], halo_t.at[layer, 1, pl.ds(0, 32)]),
            (corner_m.at[layer], halo_t.at[layer, 0, pl.ds(0, 32)]),
        )[k]
        return remote(src, dst, 11 * layer + k, peers[k][0])

    def start(layer, *numbers):
        for k in numbers:
            when(peers[k][1], lambda: copy(layer, k).start())

    def wait_recv(layer, *numbers):
        for k in numbers:
            condition = {2: not_top, 3: not_top, 4: not_top, 5: not_bottom, 6: not_bottom, 7: not_bottom}.get(k, peers[k][1])
            when(condition, lambda: copy(layer, k).wait_recv())

    def wait_sends(layer):
        for k in range(11):
            when(peers[k][1], lambda: copy(layer, k).wait_send())

    lane = ids((C, COLS), 1)

    def loop(count, body, unroll=1):
        def step(i, carry):
            body(i)
            return carry

        lax.fori_loop(0, count, step, 0, unroll=unroll)

    def add_pack(layer, rows, fresh=False):
        acc = None if fresh else pack[layer]
        for r in rows:
            turned = pltpu.roll(x_ext[layer, 3 + r], 8 * r + 3, axis=1)
            acc = turned if acc is None else jnp.where(lane // 8 == r, turned, acc)
        pack[layer] = acc

    def pick_lanes(rows, total):
        at, lanes = ids((rows, COLS), 0), ids((rows, COLS), 1)
        wanted = at if total is None else (total + COLS - at) % COLS
        return jnp.where(lanes == wanted, 1.0, 0.0).astype(BF)

    def fill_corner(layer):
        wide = jnp.concatenate([pack[layer], jnp.zeros((COLS - C, COLS), BF)], axis=0)

        def pick(rows, total):
            return lax.dot_general(
                pick_lanes(rows, total), wide, (((1,), (1,)), ((), ())), preferred_element_type=F32
            ).astype(BF)

        corner[layer] = pick(COLS, None)

        @pl.when(at_top)
        def _():
            corner_m[layer] = pick(32, 125)

        @pl.when(at_top & (fold_r == lon))
        def _():
            halo_t[layer, 1, 0:32] = corner_m[layer]

        @pl.when(at_top & (fold_l == lon))
        def _():
            halo_t[layer, 0, 0:32] = corner_m[layer]

    def send_low(layer):
        start(layer, 2)

    def send_high(layer):
        start(layer, 5)

        @pl.when(at_top)
        def _():
            flip = jnp.where(ids((COLS, COLS), 0) + ids((COLS, COLS), 1) == COLS - 1, 1.0, 0.0).astype(BF)
            rows = x_ext[layer, 16:19].reshape(3 * C, COLS)
            got = jnp.dot(rows, flip, preferred_element_type=F32).astype(BF)
            for r in range(3):
                mirror[layer, r] = got[(2 - r) * C : (3 - r) * C]
            copy(layer, 8).start()

    def send_pack(layer):
        start(layer, 0, 1)
        fill_corner(layer)
        start(layer, 3, 4, 6, 7, 9, 10)

    def take_pack(layer):
        wait_recv(layer, 0, 1)
        q_mid[layer] = jnp.where(lane % 8 >= 3, pack_r[layer], pack_l[layer])

    def take_corners(layer):
        wait_recv(layer, 3, 4, 6, 7, 9, 10)
        at = ids((COLS, COLS), 0)
        low = jnp.where(not_bottom, 96, COLS)
        both = jnp.where(at % 8 >= 3, halo_t[layer, 1].astype(F32), halo_t[layer, 0].astype(F32))
        both = jnp.where((at < 32) | (at >= low), both, 0.0).astype(BF)
        pick = jnp.where(ids((C, COLS), 0) == lane, 1.0, 0.0).astype(BF)
        q_halo[layer] = lax.dot_general(pick, both, (((1,), (1,)), ((), ())), preferred_element_type=F32).astype(BF)

    def take_low(layer):
        wait_recv(layer, 5)

        @pl.when(lat == 0)
        def _():
            x_ext[layer, 0:3] = jnp.zeros((3, C, COLS), BF)

    def take_high(layer):
        wait_recv(layer, 2, 8)

    def build_weights(layer):
        table[...] = jnp.zeros((COLS, COLS), F32)
        table[0:49, 0:C] = taps[:, layer, :]
        for k, v in enumerate((dbias, gain, nbias, b_r)):
            table[49 + k : 50 + k, 0:C] = v[layer : layer + 1, :]
        vec = jnp.transpose(table[...])[0:C]
        for k in range(4):
            colv[layer, k] = jnp.broadcast_to(vec[:, 49 + k : 50 + k], (C, COLS))
        vec = vec.astype(BF)
        bias = b_e[layer : layer + 1, :]
        high = bias.astype(BF).astype(F32)
        wide = jnp.concatenate(
            [w_e_raw[layer].astype(F32), high, bias - high, jnp.zeros((COLS - C - 2, HID), F32)], axis=0
        )
        w_e[layer] = (0.5 * jnp.transpose(wide)).astype(BF)
        shape = (COLS, 7 * COLS)
        at = ids(shape, 1)
        rest = at % COLS
        spread = jnp.where((ids(shape, 0) == (rest // 16) * 7 + at // COLS) & (rest < 112), 1.0, 0.0).astype(BF)
        flat = jnp.dot(vec, spread, preferred_element_type=F32)
        own = (lane % 16) == (ids((C, COLS), 0) % 16)
        for d in range(7):
            band = jnp.where(own, flat[:, d * COLS : (d + 1) * COLS], 0.0).astype(BF)
            none, zero = jnp.zeros_like(band), jnp.zeros((), BF)
            for r in range(ROWS):
                by = 16 * (r - 3)
                turned = band if by % COLS == 0 else pltpu.roll(band, by % COLS, axis=1)
                if by < 0:
                    low, high = jnp.where(lane < COLS + by, turned, zero), none
                elif by < COLS:
                    low, high = jnp.where(lane >= by, turned, zero), jnp.where(lane < by, turned, zero)
                else:
                    low, high = none, jnp.where(lane >= by - COLS, turned, zero)
                at_rows = slice(r * 16, (r + 1) * 16)
                conv_w[layer, :, at_rows, d * 256 : d * 256 + 128] = low.reshape(GROUPS, 16, COLS)
                conv_w[layer, :, at_rows, d * 256 + 128 : d * 256 + 256] = high.reshape(GROUPS, 16, COLS)
            for r in range(3):
                at_rows = slice(r * 16, (r + 1) * 16)
                turned = band if r == 0 else pltpu.roll(band, 16 * r, axis=1)
                part = jnp.where((lane >= 16 * r) & (lane < 48), turned, zero)
                low_w[layer, :, at_rows, d * 128 : d * 128 + 128] = part.reshape(GROUPS, 16, COLS)
                turned = band if r == 1 else pltpu.roll(band, (16 * r - 16) % COLS, axis=1)
                part = jnp.where((lane >= 80) & (lane < (112 if r == 0 else COLS)), turned, zero)
                high_w[layer, :, at_rows, d * 128 : d * 128 + 128] = part.reshape(GROUPS, 16, COLS)
        for k, d in enumerate(SIDE):
            shape = (COLS, 7 * COLS)
            at = ids(shape, 1)
            to = at % 8
            start = to + d - 3
            if d > 3:
                reach = (to < 3) & (start >= 3) & (start < 6)
            else:
                reach = (to >= 3) & (to < 6) & (start >= 0) & (start < 3)
            pick = jnp.where((ids(shape, 0) == (at // COLS) * 7 + d) & reach, 1.0, 0.0).astype(BF)
            got = jnp.dot(vec, pick, preferred_element_type=F32)
            for a in range(7):
                side_w[layer, k * 7 + a] = got[:, a * COLS : (a + 1) * COLS]

    def shift_own(layer, r):
        x = x_ext[layer, 3 + r]
        for d in range(-3, 4):
            y = x if d == 0 else pltpu.roll(x, (COLS - d) % COLS, axis=1)
            shifted[:, d + 3, 3 + r] = y.reshape(GROUPS, 16, COLS)

    def shift_halo(layer, e, q, q_row):
        x = x_ext[layer, e]
        z = pltpu.roll(q, 2 * COLS - 3 - 8 * q_row, axis=1)
        for d in range(-3, 4):
            if d == 0:
                y = x
            else:
                outside = lane < d if d > 0 else lane >= COLS + d
                y = pltpu.roll(jnp.where(outside, z, x), (COLS - d) % COLS, axis=1)
            shifted[:, d + 3, e] = y.reshape(GROUPS, 16, COLS)

    def conv_own(layer, g):
        x = shifted[g, :, 3:19].reshape(7 * 256, COLS)
        got = jnp.dot(conv_w[layer, g], x, preferred_element_type=F32)
        mixed[:, g] = got.reshape(ROWS, 16, COLS)

    def conv_low(layer, g):
        x = shifted[g, :, 0:8].reshape(7 * 128, COLS)
        got = jnp.dot(low_w[layer, g], x, preferred_element_type=F32)
        mixed[0:3, g] += got.reshape(3, 16, COLS)

    def conv_high(layer, g):
        x = shifted[g, :, 14:22].reshape(7 * 128, COLS)
        got = jnp.dot(high_w[layer, g], x, preferred_element_type=F32)
        mixed[13:16, g] += got.reshape(3, 16, COLS)

    def fill_edge(layer):
        delta = q_mid[layer].astype(F32) - pack[layer].astype(F32)
        total = jnp.zeros((C, COLS), F32)
        for a in range(7):
            by = 8 * (a - 3)
            if by > 0:
                rows = jnp.where(lane < by, 0.0, delta)
            elif by < 0:
                rows = jnp.where(lane >= COLS + by, 0.0, delta)
            else:
                rows = delta
            for k, d in enumerate(SIDE):
                total += side_w[layer, k * 7 + a] * pltpu.roll(rows, (3 * COLS - by - (d - 3)) % COLS, axis=1)
        edge[...] = total

    def mlp(layer, at_rows):
        count = len(at_rows)

        def each(pick):
            return jnp.concatenate([pick(r) for r in at_rows], axis=1)

        def same(v):
            return jnp.concatenate([v] * count, axis=1)

        def mixed_row(r):
            beside = pltpu.roll(edge[...], (2 * COLS - 3 - 8 * r) % COLS, axis=1)
            return mixed[r].reshape(C, COLS) + jnp.where((lane < 3) | (lane >= COLS - 3), beside, 0.0)

        c = each(mixed_row) + same(colv[layer, 0])
        mean = jnp.sum(c, axis=0, keepdims=True) * (1.0 / C)
        c = c - mean
        var = jnp.sum(c * c, axis=0, keepdims=True) * (1.0 / C)
        n = c * lax.rsqrt(var + 1e-6) * same(colv[layer, 1]) + same(colv[layer, 2])
        ones = jnp.where(ids((32, count * COLS), 0) < 2, 1.0, 0.0)
        n = jnp.concatenate([n, ones], axis=0).astype(BF)
        half = jnp.dot(w_e[layer], n, preferred_element_type=F32)
        h = (half + half * lax.erf(half * np.float32(np.sqrt(2.0)))).astype(BF)
        u = jnp.dot(w_r[layer], h, preferred_element_type=F32) + same(colv[layer, 3])
        x = each(lambda r: x_ext[layer, 3 + r]).astype(F32)
        flags = each(lambda r: mask[r : r + 1, :]).astype(F32)
        y = flags * (x + u)
        for k, r in enumerate(at_rows):
            part = y[:, k * COLS : (k + 1) * COLS]
            if layer == LAYERS - 1:
                cells[pl.ds(r, C, stride=ROWS), :] = part
            else:
                x_ext[layer + 1, 3 + r] = part.astype(BF)

    loads[0].wait()
    cells[...] = raw[...].astype(F32).reshape(C * ROWS, COLS)
    for r in range(ROWS):
        x_ext[0, 3 + r] = cells[pl.ds(r, C, stride=ROWS), :].astype(BF)
    add_pack(0, range(ROWS), fresh=True)
    pl.semaphore_wait(barrier, n_peers)
    send_low(0)
    send_high(0)
    send_pack(0)
    for one in loads[1:]:
        one.wait()
    for layer in range(LAYERS):
        build_weights(layer)
    for layer in range(LAYERS):
        onward = layer + 1 < LAYERS
        loop(ROWS, lambda r: shift_own(layer, r), 4)
        loop(GROUPS, lambda g: conv_own(layer, g), GROUPS)
        take_pack(layer)
        fill_edge(layer)
        for r in range(3, 13, 2):
            mlp(layer, (r, r + 1))
        if onward:
            add_pack(layer + 1, range(3, 13), fresh=True)
        take_corners(layer)
        take_low(layer)
        for e in range(3):
            shift_halo(layer, e, q_halo[layer], 13 + e)
        loop(GROUPS, lambda g: conv_low(layer, g), GROUPS)
        mlp(layer, (0, 1, 2))
        if onward:
            send_low(layer + 1)
        take_high(layer)
        for e in range(3):
            shift_halo(layer, 19 + e, q_halo[layer], e)
        loop(GROUPS, lambda g: conv_high(layer, g), GROUPS)
        mlp(layer, (13, 14, 15))
        if onward:
            send_high(layer + 1)
            add_pack(layer + 1, (0, 1, 2, 13, 14, 15))
            send_pack(layer + 1)
    out[...] = cells[...].reshape(C, ROWS, COLS).astype(BF)
    for layer in range(LAYERS):
        wait_sends(layer)


def per_device(
    field, land_mask, depth_kernel, depth_bias, norm_gain, norm_bias, w_expand, b_expand, w_reduce, b_reduce
):
    taps = jnp.transpose(depth_kernel, (2, 3, 0, 1)).reshape(49, LAYERS, C)
    args = (
        field, land_mask, taps, depth_bias, norm_gain, norm_bias, jnp.transpose(w_expand, (0, 2, 1)), b_expand,
        w_reduce, b_reduce,
    )
    tile = (LAYERS, C, COLS)
    held = [pltpu.VMEM(a.shape, a.dtype) for a in args]
    scratch = held + [
        pltpu.VMEM((C * ROWS, COLS), F32),
        pltpu.VMEM((LAYERS, ROWS + 6, C, COLS), BF),
    ]
    scratch += [pltpu.VMEM(tile, BF)] * 5
    scratch += [
        pltpu.VMEM((LAYERS, 3, C, COLS), BF),
        pltpu.VMEM((LAYERS, COLS, COLS), BF),
        pltpu.VMEM((LAYERS, 32, COLS), BF),
        pltpu.VMEM((LAYERS, 2, COLS, COLS), BF),
        pltpu.VMEM((COLS, COLS), F32),
        pltpu.VMEM((LAYERS, HID, COLS), BF),
        pltpu.VMEM((LAYERS, GROUPS, 256, 7 * 256), BF),
        pltpu.VMEM((LAYERS, GROUPS, 48, 7 * 128), BF),
        pltpu.VMEM((LAYERS, GROUPS, 48, 7 * 128), BF),
        pltpu.VMEM((LAYERS, 42, C, COLS), F32),
        pltpu.VMEM((LAYERS, 4, C, COLS), F32),
        pltpu.VMEM((GROUPS, 7, ROWS + 6, 16, COLS), BF),
        pltpu.VMEM((ROWS, GROUPS, 16, COLS), F32),
        pltpu.VMEM((C, COLS), F32),
        pltpu.SemaphoreType.DMA((len(args),)),
        pltpu.SemaphoreType.DMA((11 * LAYERS,)),
        pltpu.SemaphoreType.DMA((11 * LAYERS,)),
    ]
    return pl.pallas_call(
        kernel,
        out_shape=jax.ShapeDtypeStruct((C, ROWS, COLS), BF),
        in_specs=[pl.BlockSpec(memory_space=pltpu.HBM)] * len(args),
        out_specs=pl.BlockSpec(memory_space=pltpu.VMEM),
        scratch_shapes=scratch,
        compiler_params=pltpu.CompilerParams(
            collective_id=0, has_side_effects=True, vmem_limit_bytes=40 * 1024 * 1024
        ),
    )(*[pltpu.with_memory_space_constraint(a, pltpu.HBM) for a in args])


def solution(mesh):
    placed = (P(None, "lat", "lon"), P("lat", "lon"), P(), P(), P(), P(), P(), P(), P(), P())
    return jax.shard_map(
        per_device, mesh=mesh, in_specs=placed, out_specs=P(None, "lat", "lon"), check_vma=False
    )
```

time: 39.2 us -> 36.6 us (0.934)
  Pallas kernels: 37.3 us -> 35.7 us
  local copies, waits for them, and re-layouts: 1.77 us -> 0.75 us
    pallas_call x1, Pallas kernels: 37.3 us -> 35.7 us  [per_device(): pl.pallas_call(kernel, out_shape=jax.ShapeDtypeStruct((C, ROWS, COLS), BF...]
    unnamed x1, local copies, waits for them, and re-layouts: 1.77 us -> 0.75 us
where the time goes in v3:
time: 36.6 us; the launch traced here: 36.5 us
  Pallas kernels  35.7 us (98%)
  local copies, waits for them, and re-layouts  0.75 us (2%)
    pallas_call x1, Pallas kernels, per_device(): pl.pallas_call(kernel, out_shape=jax.ShapeDtypeStruct((C, ROWS, COLS), BF...  35.7 us
    unnamed x1, local copies, waits for them, and re-layouts  0.75 us

profile of v3, /device:TPU:70, one launch (start us, length us, event | category | flops | bytes accessed | tf_op | source)
XLA Modules:
  0.0 36.5 jit_solution(2927926612439590042)
XLA Ops:
  0.0 35.7 %shard_map.100 = bf16[96,16,128]{2,1,0:T(8,128)(2,1)S(1)} custom-call(bf16[96,16,128]{2,1,0:T(8,128)(2,1)} %field.1, s32[16,128]{1,0:T(8,128)} %mask_in.1, f32[49,2,96]{2,1,0:T(2,128)} %bitcast.5, f32[2,96]{1,0:T(2,128)} %dbias_in.1, f32[2,96]{1,0:T(2,128)} %gain_in.1, f32[2,96]{1,0:T(2,128)} %nbias_in.1, bf16[2,96,384]{2,1,0:T(8,128)(2,1)} %bitcast.4, ...), custom_call_target="tpu_custom_call" | custom-call | tf_op jit(solution)/shard_map/pallas_call | solution.py:416
  35.7 0.7 %copy.12 = bf16[96,16,128]{2,1,0:T(8,128)(2,1)} copy(bf16[96,16,128]{2,1,0:T(8,128)(2,1)S(1)} %shard_map.100) | data formatting | bytes 786432

commit v4 on v3

--- a/solution.py
+++ b/solution.py
@@ -26,7 +26,7 @@
     field, mask_in, taps_in, dbias_in, gain_in, nbias_in, w_e_in, b_e_in, w_r_in, b_r_in, out,
     raw, mask, taps, dbias, gain, nbias, w_e_raw, b_e, w_r, b_r,
     cells, x_ext, pack, pack_l, pack_r, q_mid, q_halo, mirror, corner, corner_m, halo_t,
-    table, w_e, conv_w, low_w, high_w, side_w, colv, shifted, mixed, edge, load, send, recv,
+    table, w_e, conv_w, tap_w, colv, shifted, mixed, edge, load, send, recv,
 ):
     lat, lon = lax.axis_index("lat"), lax.axis_index("lon")
     nlat, nlon = lax.axis_size("lat"), lax.axis_size("lon")
@@ -170,6 +170,8 @@
 
     def send_pack(layer):
         start(layer, 0, 1)
+
+    def send_corners(layer):
         fill_corner(layer)
         start(layer, 3, 4, 6, 7, 9, 10)
 
@@ -217,42 +219,20 @@
         spread = jnp.where((ids(shape, 0) == (rest // 16) * 7 + at // COLS) & (rest < 112), 1.0, 0.0).astype(BF)
         flat = jnp.dot(vec, spread, preferred_element_type=F32)
         own = (lane % 16) == (ids((C, COLS), 0) % 16)
+        zero = jnp.zeros((), BF)
         for d in range(7):
             band = jnp.where(own, flat[:, d * COLS : (d + 1) * COLS], 0.0).astype(BF)
-            none, zero = jnp.zeros_like(band), jnp.zeros((), BF)
-            for r in range(ROWS):
-                by = 16 * (r - 3)
-                turned = band if by % COLS == 0 else pltpu.roll(band, by % COLS, axis=1)
-                if by < 0:
-                    low, high = jnp.where(lane < COLS + by, turned, zero), none
-                elif by < COLS:
-                    low, high = jnp.where(lane >= by, turned, zero), jnp.where(lane < by, turned, zero)
-                else:
-                    low, high = none, jnp.where(lane >= by - COLS, turned, zero)
+            for r in range(8):
+                by = 16 * r
+                turned = band if r == 0 else pltpu.roll(band, by, axis=1)
+                low = jnp.where(lane >= by, turned, zero)
+                high = jnp.where(lane < by, turned, zero)
                 at_rows = slice(r * 16, (r + 1) * 16)
                 conv_w[layer, :, at_rows, d * 256 : d * 256 + 128] = low.reshape(GROUPS, 16, COLS)
                 conv_w[layer, :, at_rows, d * 256 + 128 : d * 256 + 256] = high.reshape(GROUPS, 16, COLS)
-            for r in range(3):
-                at_rows = slice(r * 16, (r + 1) * 16)
-                turned = band if r == 0 else pltpu.roll(band, 16 * r, axis=1)
-                part = jnp.where((lane >= 16 * r) & (lane < 48), turned, zero)
-                low_w[layer, :, at_rows, d * 128 : d * 128 + 128] = part.reshape(GROUPS, 16, COLS)
-                turned = band if r == 1 else pltpu.roll(band, (16 * r - 16) % COLS, axis=1)
-                part = jnp.where((lane >= 80) & (lane < (112 if r == 0 else COLS)), turned, zero)
-                high_w[layer, :, at_rows, d * 128 : d * 128 + 128] = part.reshape(GROUPS, 16, COLS)
-        for k, d in enumerate(SIDE):
-            shape = (COLS, 7 * COLS)
-            at = ids(shape, 1)
-            to = at % 8
-            start = to + d - 3
-            if d > 3:
-                reach = (to < 3) & (start >= 3) & (start < 6)
-            else:
-                reach = (to >= 3) & (to < 6) & (start >= 0) & (start < 3)
-            pick = jnp.where((ids(shape, 0) == (at // COLS) * 7 + d) & reach, 1.0, 0.0).astype(BF)
-            got = jnp.dot(vec, pick, preferred_element_type=F32)
-            for a in range(7):
-                side_w[layer, k * 7 + a] = got[:, a * COLS : (a + 1) * COLS]
+        rounded = vec.astype(F32)
+        for k in range(49):
+            tap_w[layer, k] = jnp.broadcast_to(rounded[:, k : k + 1], (C, COLS))
 
     def shift_own(layer, r):
         x = x_ext[layer, 3 + r]
@@ -260,35 +240,42 @@
             y = x if d == 0 else pltpu.roll(x, (COLS - d) % COLS, axis=1)
             shifted[:, d + 3, 3 + r] = y.reshape(GROUPS, 16, COLS)
 
-    def shift_halo(layer, e, q, q_row):
-        x = x_ext[layer, e]
-        z = pltpu.roll(q, 2 * COLS - 3 - 8 * q_row, axis=1)
-        for d in range(-3, 4):
-            if d == 0:
-                y = x
-            else:
-                outside = lane < d if d > 0 else lane >= COLS + d
-                y = pltpu.roll(jnp.where(outside, z, x), (COLS - d) % COLS, axis=1)
-            shifted[:, d + 3, e] = y.reshape(GROUPS, 16, COLS)
-
     def conv_own(layer, g):
-        x = shifted[g, :, 3:19].reshape(7 * 256, COLS)
+        x = jnp.concatenate(
+            [shifted[g, :, 0:16].reshape(7 * 256, COLS), shifted[g, :, 8:24].reshape(7 * 256, COLS)], axis=1
+        )
         got = jnp.dot(conv_w[layer, g], x, preferred_element_type=F32)
-        mixed[:, g] = got.reshape(ROWS, 16, COLS)
-
-    def conv_low(layer, g):
-        x = shifted[g, :, 0:8].reshape(7 * 128, COLS)
-        got = jnp.dot(low_w[layer, g], x, preferred_element_type=F32)
-        mixed[0:3, g] += got.reshape(3, 16, COLS)
-
-    def conv_high(layer, g):
-        x = shifted[g, :, 14:22].reshape(7 * 128, COLS)
-        got = jnp.dot(high_w[layer, g], x, preferred_element_type=F32)
-        mixed[13:16, g] += got.reshape(3, 16, COLS)
+        for k in range(2):
+            mixed[8 * k : 8 * k + 8, g] = got[:, k * COLS : (k + 1) * COLS].reshape(8, 16, COLS)
+
+    def halo_rows(layer, upper):
+        some = lane[0:16]
+        for g in range(GROUPS):
+            at = slice(16 * g, 16 * g + 16)
+            q = q_halo[layer, at].astype(F32)
+            total = [jnp.zeros((16, COLS), F32)] * 3
+            x, z = [], []
+            for k in range(3):
+                x.append(x_ext[layer, (19 if upper else 0) + k, at].astype(F32))
+                z.append(pltpu.roll(q, 2 * COLS - 3 - 8 * (k if upper else 13 + k), axis=1))
+            for d in range(7):
+                by = d - 3
+                for k in range(3):
+                    if by == 0:
+                        y = x[k]
+                    else:
+                        outside = some < by if by > 0 else some >= COLS + by
+                        y = pltpu.roll(jnp.where(outside, z[k], x[k]), (COLS - by) % COLS, axis=1)
+                    for r in range(3):
+                        a = 6 + k - r if upper else k - r
+                        if 0 <= a < 7:
+                            total[r] = total[r] + tap_w[layer, a * 7 + d, at] * y
+            for r in range(3):
+                mixed[(13 if upper else 0) + r, g] += total[r]
 
     def fill_edge(layer):
         delta = q_mid[layer].astype(F32) - pack[layer].astype(F32)
-        total = jnp.zeros((C, COLS), F32)
+        parts = [jnp.zeros((C, COLS), F32) for _ in SIDE]
         for a in range(7):
             by = 8 * (a - 3)
             if by > 0:
@@ -298,7 +285,16 @@
             else:
                 rows = delta
             for k, d in enumerate(SIDE):
-                total += side_w[layer, k * 7 + a] * pltpu.roll(rows, (3 * COLS - by - (d - 3)) % COLS, axis=1)
+                parts[k] += tap_w[layer, a * 7 + d] * pltpu.roll(rows, (3 * COLS - by - (d - 3)) % COLS, axis=1)
+        to = lane % 8
+        total = jnp.zeros((C, COLS), F32)
+        for part, d in zip(parts, SIDE):
+            start = to + d - 3
+            if d > 3:
+                reach = (to < 3) & (start >= 3) & (start < 6)
+            else:
+                reach = (to >= 3) & (to < 6) & (start >= 0) & (start < 3)
+            total = total + jnp.where(reach, part, 0.0)
         edge[...] = total
 
     def mlp(layer, at_rows):
@@ -339,40 +335,46 @@
     for r in range(ROWS):
         x_ext[0, 3 + r] = cells[pl.ds(r, C, stride=ROWS), :].astype(BF)
     add_pack(0, range(ROWS), fresh=True)
+    for rows in (slice(0, 3), slice(19, 24)):
+        shifted[:, :, rows] = jnp.zeros((GROUPS, 7, rows.stop - rows.start, 16, COLS), BF)
     pl.semaphore_wait(barrier, n_peers)
     send_low(0)
     send_high(0)
     send_pack(0)
+    send_corners(0)
     for one in loads[1:]:
         one.wait()
-    for layer in range(LAYERS):
-        build_weights(layer)
+    build_weights(0)
+
+    def interior(layer):
+        for r in range(3, 13, 2):
+            mlp(layer, (r, r + 1))
+
     for layer in range(LAYERS):
         onward = layer + 1 < LAYERS
-        loop(ROWS, lambda r: shift_own(layer, r), 4)
+        loop(ROWS, lambda r: shift_own(layer, r), ROWS)
         loop(GROUPS, lambda g: conv_own(layer, g), GROUPS)
         take_pack(layer)
         fill_edge(layer)
-        for r in range(3, 13, 2):
-            mlp(layer, (r, r + 1))
         if onward:
-            add_pack(layer + 1, range(3, 13), fresh=True)
+            build_weights(layer + 1)
+        else:
+            interior(layer)
         take_corners(layer)
         take_low(layer)
-        for e in range(3):
-            shift_halo(layer, e, q_halo[layer], 13 + e)
-        loop(GROUPS, lambda g: conv_low(layer, g), GROUPS)
+        halo_rows(layer, False)
         mlp(layer, (0, 1, 2))
         if onward:
             send_low(layer + 1)
         take_high(layer)
-        for e in range(3):
-            shift_halo(layer, 19 + e, q_halo[layer], e)
-        loop(GROUPS, lambda g: conv_high(layer, g), GROUPS)
+        halo_rows(layer, True)
         mlp(layer, (13, 14, 15))
         if onward:
             send_high(layer + 1)
-            add_pack(layer + 1, (0, 1, 2, 13, 14, 15))
+            add_pack(layer + 1, (0, 1, 2, 13, 14, 15), fresh=True)
+            send_corners(layer + 1)
+            interior(layer)
+            add_pack(layer + 1, range(3, 13))
             send_pack(layer + 1)
     out[...] = cells[...].reshape(C, ROWS, COLS).astype(BF)
     for layer in range(LAYERS):
@@ -401,12 +403,10 @@
         pltpu.VMEM((LAYERS, 2, COLS, COLS), BF),
         pltpu.VMEM((COLS, COLS), F32),
         pltpu.VMEM((LAYERS, HID, COLS), BF),
-        pltpu.VMEM((LAYERS, GROUPS, 256, 7 * 256), BF),
-        pltpu.VMEM((LAYERS, GROUPS, 48, 7 * 128), BF),
-        pltpu.VMEM((LAYERS, GROUPS, 48, 7 * 128), BF),
-        pltpu.VMEM((LAYERS, 42, C, COLS), F32),
+        pltpu.VMEM((LAYERS, GROUPS, COLS, 7 * 256), BF),
+        pltpu.VMEM((LAYERS, 49, C, COLS), F32),
         pltpu.VMEM((LAYERS, 4, C, COLS), F32),
-        pltpu.VMEM((GROUPS, 7, ROWS + 6, 16, COLS), BF),
+        pltpu.VMEM((GROUPS, 7, ROWS + 8, 16, COLS), BF),
         pltpu.VMEM((ROWS, GROUPS, 16, COLS), F32),
         pltpu.VMEM((C, COLS), F32),
         pltpu.SemaphoreType.DMA((len(args),)),

time: 36.6 us -> 35.4 us (0.967)
  the two profiles are of different devices: /device:TPU:70 before, /device:TPU:6 now
where the time goes in v4:
time: 35.4 us; the launch traced here: 35.1 us
  Pallas kernels  34.3 us (97%)
  local copies, waits for them, and re-layouts  0.75 us (2%)
    pallas_call x1, Pallas kernels, per_device(): pl.pallas_call(kernel, out_shape=jax.ShapeDtypeStruct((C, ROWS, COLS), BF...  34.3 us
    unnamed x1, local copies, waits for them, and re-layouts  0.75 us

profile of v4, /device:TPU:6, one launch (start us, length us, event | category | flops | bytes accessed | tf_op | source)
XLA Modules:
  0.0 35.1 jit_solution(13114676435794492540)
XLA Ops:
  0.0 34.3 %shard_map.100 = bf16[96,16,128]{2,1,0:T(8,128)(2,1)S(1)} custom-call(bf16[96,16,128]{2,1,0:T(8,128)(2,1)} %field.1, s32[16,128]{1,0:T(8,128)} %mask_in.1, f32[49,2,96]{2,1,0:T(2,128)} %bitcast.5, f32[2,96]{1,0:T(2,128)} %dbias_in.1, f32[2,96]{1,0:T(2,128)} %gain_in.1, f32[2,96]{1,0:T(2,128)} %nbias_in.1, bf16[2,96,384]{2,1,0:T(8,128)(2,1)} %bitcast.4, ...), custom_call_target="tpu_custom_call" | custom-call | tf_op jit(solution)/shard_map/pallas_call | solution.py:416
  34.3 0.7 %copy.12 = bf16[96,16,128]{2,1,0:T(8,128)(2,1)} copy(bf16[96,16,128]{2,1,0:T(8,128)(2,1)S(1)} %shard_map.100) | data formatting | bytes 786432

commit v5 on v4

--- a/solution.py
+++ b/solution.py
@@ -156,9 +156,7 @@
     def send_low(layer):
         start(layer, 2)
 
-    def send_high(layer):
-        start(layer, 5)
-
+    def fill_mirror(layer):
         @pl.when(at_top)
         def _():
             flip = jnp.where(ids((COLS, COLS), 0) + ids((COLS, COLS), 1) == COLS - 1, 1.0, 0.0).astype(BF)
@@ -166,7 +164,9 @@
             got = jnp.dot(rows, flip, preferred_element_type=F32).astype(BF)
             for r in range(3):
                 mirror[layer, r] = got[(2 - r) * C : (3 - r) * C]
-            copy(layer, 8).start()
+
+    def send_high(layer):
+        start(layer, 5, 8)
 
     def send_pack(layer):
         start(layer, 0, 1)
@@ -332,16 +332,22 @@
 
     loads[0].wait()
     cells[...] = raw[...].astype(F32).reshape(C * ROWS, COLS)
-    for r in range(ROWS):
-        x_ext[0, 3 + r] = cells[pl.ds(r, C, stride=ROWS), :].astype(BF)
+
+    def take_rows(rows):
+        for r in rows:
+            x_ext[0, 3 + r] = cells[pl.ds(r, C, stride=ROWS), :].astype(BF)
+
+    take_rows((0, 1, 2, 13, 14, 15))
+    fill_mirror(0)
+    take_rows(range(3, 13))
     add_pack(0, range(ROWS), fresh=True)
+    pl.semaphore_wait(barrier, n_peers)
+    send_pack(0)
+    send_high(0)
+    send_low(0)
+    send_corners(0)
     for rows in (slice(0, 3), slice(19, 24)):
         shifted[:, :, rows] = jnp.zeros((GROUPS, 7, rows.stop - rows.start, 16, COLS), BF)
-    pl.semaphore_wait(barrier, n_peers)
-    send_low(0)
-    send_high(0)
-    send_pack(0)
-    send_corners(0)
     for one in loads[1:]:
         one.wait()
     build_weights(0)
@@ -356,26 +362,24 @@
         loop(GROUPS, lambda g: conv_own(layer, g), GROUPS)
         take_pack(layer)
         fill_edge(layer)
+        interior(layer)
         if onward:
-            build_weights(layer + 1)
-        else:
-            interior(layer)
+            add_pack(layer + 1, range(3, 13), fresh=True)
         take_corners(layer)
         take_low(layer)
+        take_high(layer)
         halo_rows(layer, False)
+        halo_rows(layer, True)
         mlp(layer, (0, 1, 2))
-        if onward:
-            send_low(layer + 1)
-        take_high(layer)
-        halo_rows(layer, True)
         mlp(layer, (13, 14, 15))
         if onward:
+            fill_mirror(layer + 1)
+            add_pack(layer + 1, (0, 1, 2, 13, 14, 15))
+            send_pack(layer + 1)
             send_high(layer + 1)
-            add_pack(layer + 1, (0, 1, 2, 13, 14, 15), fresh=True)
+            send_low(layer + 1)
             send_corners(layer + 1)
-            interior(layer)
-            add_pack(layer + 1, range(3, 13))
-            send_pack(layer + 1)
+            build_weights(layer + 1)
     out[...] = cells[...].reshape(C, ROWS, COLS).astype(BF)
     for layer in range(LAYERS):
         wait_sends(layer)

time: 35.4 us -> 32.3 us (0.912)
  Pallas kernels: 34.3 us -> 31.4 us
    pallas_call x1, Pallas kernels: 34.3 us -> 31.4 us  [per_device(): pl.pallas_call(kernel, out_shape=jax.ShapeDtypeStruct((C, ROWS, COLS), BF...]
where the time goes in v5:
time: 32.3 us; the launch traced here: 32.2 us
  Pallas kernels  31.4 us (97%)
  local copies, waits for them, and re-layouts  0.75 us (2%)
    pallas_call x1, Pallas kernels, per_device(): pl.pallas_call(kernel, out_shape=jax.ShapeDtypeStruct((C, ROWS, COLS), BF...  31.4 us
    unnamed x1, local copies, waits for them, and re-layouts  0.75 us

profile of v5, /device:TPU:6, one launch (start us, length us, event | category | flops | bytes accessed | tf_op | source)
XLA Modules:
  0.0 32.2 jit_solution(15087521844179084059)
XLA Ops:
  0.0 31.4 %shard_map.100 = bf16[96,16,128]{2,1,0:T(8,128)(2,1)S(1)} custom-call(bf16[96,16,128]{2,1,0:T(8,128)(2,1)} %field.1, s32[16,128]{1,0:T(8,128)} %mask_in.1, f32[49,2,96]{2,1,0:T(2,128)} %bitcast.5, f32[2,96]{1,0:T(2,128)} %dbias_in.1, f32[2,96]{1,0:T(2,128)} %gain_in.1, f32[2,96]{1,0:T(2,128)} %nbias_in.1, bf16[2,96,384]{2,1,0:T(8,128)(2,1)} %bitcast.4, ...), custom_call_target="tpu_custom_call" | custom-call | tf_op jit(solution)/shard_map/pallas_call | solution.py:420
  31.4 0.7 %copy.12 = bf16[96,16,128]{2,1,0:T(8,128)(2,1)} copy(bf16[96,16,128]{2,1,0:T(8,128)(2,1)S(1)} %shard_map.100) | data formatting | bytes 786432

commit v6 on v5

--- a/solution.py
+++ b/solution.py
@@ -373,9 +373,9 @@
         mlp(layer, (0, 1, 2))
         mlp(layer, (13, 14, 15))
         if onward:
-            fill_mirror(layer + 1)
             add_pack(layer + 1, (0, 1, 2, 13, 14, 15))
             send_pack(layer + 1)
+            fill_mirror(layer + 1)
             send_high(layer + 1)
             send_low(layer + 1)
             send_corners(layer + 1)

time: 32.3 us -> 32.3 us (level)
  no operation moved by 1% of the time
where the time goes in v6:
time: 32.3 us; the launch traced here: 32.2 us
  Pallas kernels  31.4 us (97%)
  local copies, waits for them, and re-layouts  0.75 us (2%)
    pallas_call x1, Pallas kernels, per_device(): pl.pallas_call(kernel, out_shape=jax.ShapeDtypeStruct((C, ROWS, COLS), BF...  31.4 us
    unnamed x1, local copies, waits for them, and re-layouts  0.75 us

profile of v6, /device:TPU:6, one launch (start us, length us, event | category | flops | bytes accessed | tf_op | source)
XLA Modules:
  0.0 32.2 jit_solution(2394963765093728049)
XLA Ops:
  0.0 31.4 %shard_map.100 = bf16[96,16,128]{2,1,0:T(8,128)(2,1)S(1)} custom-call(bf16[96,16,128]{2,1,0:T(8,128)(2,1)} %field.1, s32[16,128]{1,0:T(8,128)} %mask_in.1, f32[49,2,96]{2,1,0:T(2,128)} %bitcast.5, f32[2,96]{1,0:T(2,128)} %dbias_in.1, f32[2,96]{1,0:T(2,128)} %gain_in.1, f32[2,96]{1,0:T(2,128)} %nbias_in.1, bf16[2,96,384]{2,1,0:T(8,128)(2,1)} %bitcast.4, ...), custom_call_target="tpu_custom_call" | custom-call | tf_op jit(solution)/shard_map/pallas_call | solution.py:420
  31.4 0.7 %copy.12 = bf16[96,16,128]{2,1,0:T(8,128)(2,1)} copy(bf16[96,16,128]{2,1,0:T(8,128)(2,1)S(1)} %shard_map.100) | data formatting | bytes 786432
